TPU v7x, 32 devices: a whole 2x2x4 slice. The times are simulated.
32 devices in a mesh: sec: 2 (over y), gx: 4 (over z), gy: 4 (over x, core).
Axes of the slice: x: 2, y: 2, z: 4, core: 2. Of those that a mesh axis runs over, the one named last changes fastest.
Arguments:
- model_state: float32 [2, 3, 32, 64, 2048], P('sec', None, None, 'gx', 'gy'), may hold values from -6 to 6
- wave_speed: float32 [2, 64, 2048], P('sec', 'gx', 'gy'), may hold values from 0.05 to 0.45
- wet_mask: int32 [2, 64, 2048], P('sec', 'gx', 'gy'), may hold values 0 or 1
- vertical: float32 [2, 32, 32], P('sec'), may hold values from -1 to 1
- surface_temp: float32 [2, 64, 2048], P('sec', 'gx', 'gy'), may hold values from -6 to 6
- flux_coef: float32 [8, 4], replicated, may hold values from -3 to 3
- heat_gain: float32 [8], replicated, may hold values from -2.5 to 2.5
- pair_tile: int32 [4, 4, 64, 1], P('gx', 'gy'), may hold values from 0 to 3; in each aligned block of 64 rows (0 to 63, 64 to 127, ..., all dimensions but the last counted through in order) at most 32 rows name the same one
- pair_source: int32 [4, 4, 64], P('gx', 'gy'), may hold values from 0 to 31
- pair_target: int32 [4, 4, 64], P('gx', 'gy'), may hold values from 0 to 63
- intersection_weights: bfloat16 [4, 4, 64, 256, 128], P('gx', 'gy'), may hold values from -0.375 to 0.375
Outputs:
- final_state: float32 [2, 3, 32, 64, 2048], P('sec', None, None, 'gx', 'gy')
- surface_temps: float32 [2, 64, 2048], P('sec', 'gx', 'gy')
Inputs may be any that keep to these rules, and one draw needn't show every extreme that they name: `pair_tile`: the destination lies in the source tile's column along gy; at most 32 pairs of one atmosphere tile name one ocean tile, and in some tile exactly 32 do.
All inputs are finite; a program needn't handle non-finite values. No bound on the sum of `wet_mask` on one device may be relied on, other than what follows from the above.
Results may differ from a plain program's by a relative error of at most 0.0033.
Values may be sent and summed in bfloat16 or wider, within the bound.
A program may use at most 64 MiB of HBM per device.

v0:
```python
import jax
import jax.numpy as jnp
from jax import lax
from jax.sharding import PartitionSpec as P

SUBSTEPS = 2


HIGHEST_PRECISION = lax.Precision.HIGHEST


def extended(cells, sides, width):
    for axis, dim in sides:
        count = lax.axis_size(axis)
        ends = count - 1
        head = lax.slice_in_dim(cells, 0, width, axis=dim)
        tail = lax.slice_in_dim(cells, cells.shape[dim] - width, cells.shape[dim], axis=dim)
        cells = jnp.concatenate(
            [
                lax.ppermute(tail, axis, [(i, (i + 1) % count) for i in range(ends)]),
                cells,
                lax.ppermute(head, axis, [((i + 1) % count, i) for i in range(ends)]),
            ],
            axis=dim,
        )
    return cells


def shifted_2(value, axis, by):
    size = lax.axis_size(axis)
    pairs = [(i, i + by) for i in range(size) if 0 <= i + by < size]
    return lax.ppermute(value, axis, pairs)


def vertical_mix(matrix, right_side):
    return right_side + jnp.einsum("lm,mxy->lxy", matrix, right_side, precision=HIGHEST_PRECISION)


def substeps_deep(pressure, eastward, northward, sound_speed, wetness, matrix):
    levels = pressure.shape[0]
    stacked = jnp.concatenate(
        [pressure, eastward, northward, sound_speed[None], wetness[None]], axis=0
    )
    widened = extended(stacked, (("gx", 1), ("gy", 2)), 2 * SUBSTEPS)
    pressure = widened[:levels]
    eastward = widened[levels : 2 * levels]
    northward = widened[2 * levels : 3 * levels]
    sound_speed = widened[3 * levels]
    wetness = widened[3 * levels + 1]
    for substep in range(SUBSTEPS):
        divergence = (
            eastward[:, 2:, 1:-1]
            - eastward[:, :-2, 1:-1]
            + (northward[:, 1:-1, 2:] - northward[:, 1:-1, :-2])
        )
        right_side = pressure[:, 1:-1, 1:-1] - sound_speed[1:-1, 1:-1] * divergence
        pressure_new = vertical_mix(matrix, right_side)
        wetness = wetness[2:-2, 2:-2]
        eastward = wetness * (
            eastward[:, 2:-2, 2:-2] - 0.5 * (pressure_new[:, 2:, 1:-1] - pressure_new[:, :-2, 1:-1])
        )
        northward = wetness * (
            northward[:, 2:-2, 2:-2]
            - 0.5 * (pressure_new[:, 1:-1, 2:] - pressure_new[:, 1:-1, :-2])
        )
        pressure = pressure_new[:, 1:-1, 1:-1]
        sound_speed = sound_speed[2:-2, 2:-2]
    return (pressure, eastward, northward)


def local(
    model_state,
    wave_speed,
    wet_mask,
    vertical,
    surface_temp,
    flux_coef,
    heat_gain,
    pair_tile,
    pair_source,
    pair_target,
    intersection_weights,
):
    pressure = model_state[0, 0]
    eastward = model_state[0, 1]
    northward = model_state[0, 2]
    sound_speed = wave_speed[0]
    wetness = wet_mask[0].astype(jnp.float32)
    matrix = vertical[0]
    pressure, eastward, northward = substeps_deep(
        pressure, eastward, northward, sound_speed, wetness, matrix
    )
    final_state = jnp.stack([pressure, eastward, northward])[None]
    tile_count = lax.axis_size("gx")
    weights = intersection_weights[0, 0]
    pair_count = weights.shape[0]
    in_width = weights.shape[1]
    out_width = weights.shape[2]
    capacity = max(2, 2 * pair_count // tile_count)
    slot_count = tile_count * capacity
    grid_shape = surface_temp.shape[1:]
    cell_count = grid_shape[0] * grid_shape[1]
    in_blocks = cell_count // in_width
    out_blocks = cell_count // out_width
    sources = pair_source[0, 0]
    targets = pair_target[0, 0]
    target_tile = pair_tile[0, 0, :, 0]
    drivers = jnp.stack(
        [model_state[0, 0, 0], model_state[0, 1, 0], model_state[0, 2, 0], surface_temp[0]]
    ).reshape(4, cell_count)
    fluxes = jnp.tanh(jnp.dot(flux_coef, drivers, precision=HIGHEST_PRECISION)).astype(jnp.bfloat16)
    flux_count = fluxes.shape[0]
    blocks = fluxes.reshape(flux_count, in_blocks, in_width)
    picked = jnp.take(blocks, sources, axis=1)
    regridded = jnp.einsum(
        "fpi,pio->pfo", picked, weights, preferred_element_type=jnp.float32
    ).astype(jnp.bfloat16)
    positions = jnp.arange(pair_count)
    same_tile = target_tile[None, :] == target_tile[:, None]
    is_before = positions[None, :] < positions[:, None]
    earlier = jnp.sum(same_tile & is_before, axis=1)
    slot_of = target_tile * capacity + earlier
    placing = jnp.arange(slot_count)[:, None] == slot_of[None, :]
    outgoing = jnp.dot(
        placing.astype(jnp.bfloat16),
        regridded.reshape(pair_count, flux_count * out_width),
        preferred_element_type=jnp.float32,
    )
    outgoing = outgoing.astype(jnp.bfloat16).reshape(tile_count, capacity, flux_count, out_width)
    offsets = (jnp.sum(jnp.where(placing, targets[None, :] + 1, 0), axis=1) - 1).reshape(
        tile_count, capacity
    )
    shifted = shifted_2((outgoing, offsets), "sec", 1)
    arrived, arrived_at = (
        lax.all_to_all(shifted[0], "gx", split_axis=0, concat_axis=0, tiled=True),
        lax.all_to_all(shifted[1], "gx", split_axis=0, concat_axis=0, tiled=True),
    )
    landing = jnp.arange(out_blocks)[:, None] == arrived_at.reshape(slot_count)[None, :]
    gathered = jnp.dot(
        landing.astype(jnp.bfloat16),
        arrived.reshape(slot_count, flux_count * out_width),
        preferred_element_type=jnp.float32,
    )
    ocean_flux = (
        gathered.reshape(out_blocks, flux_count, out_width)
        .transpose(1, 0, 2)
        .reshape(flux_count, cell_count)
    )
    heating = jnp.dot(heat_gain, ocean_flux, precision=HIGHEST_PRECISION).reshape(grid_shape)
    ocean_temp = surface_temp[0] + wetness * heating
    returning = jnp.dot(
        landing.T.astype(jnp.bfloat16),
        ocean_temp.astype(jnp.bfloat16).reshape(out_blocks, out_width),
        preferred_element_type=jnp.float32,
    )
    returning = returning.astype(jnp.bfloat16).reshape(tile_count, capacity, out_width)
    exchanged_back = lax.all_to_all(returning, "gx", split_axis=0, concat_axis=0, tiled=True)
    delivered = shifted_2(exchanged_back, "sec", -1)
    per_pair = jnp.dot(
        placing.T.astype(jnp.bfloat16),
        delivered.reshape(slot_count, out_width),
        preferred_element_type=jnp.float32,
    ).astype(jnp.bfloat16)
    pieces = jnp.einsum("pio,po->pi", weights, per_pair, preferred_element_type=jnp.float32)
    owning = (jnp.arange(in_blocks)[:, None] == sources[None, :]).astype(jnp.float32)
    atmos_temp = jnp.dot(owning, pieces, precision=HIGHEST_PRECISION).reshape(grid_shape)
    section = lax.axis_index("sec")
    surface_temps = jnp.where(section == 0, atmos_temp, ocean_temp)[None]
    return (final_state, surface_temps)


def solution(mesh):
    return jax.shard_map(
        local,
        mesh=mesh,
        in_specs=(
            P("sec", None, None, "gx", "gy"),
            P("sec", "gx", "gy"),
            P("sec", "gx", "gy"),
            P("sec", None, None),
            P("sec", "gx", "gy"),
            P(),
            P(),
            P("gx", "gy", None, None),
            P("gx", "gy", None),
            P("gx", "gy", None),
            P("gx", "gy", None, None, None),
        ),
        out_specs=(P("sec", None, None, "gx", "gy"), P("sec", "gx", "gy")),
        check_vma=False,
    )
```

profile of v0, /device:TPU:0, one launch (start us, length us, event | category | flops | bytes accessed | tf_op | source)
XLA Modules:
  0.0 127.3 jit_solution(16809153297405198771)
XLA Ops:
  0.6 0.7 add_bitcast_fusion
  1.3 0.9 convert_reduce_fusion
  2.2 0.7 multiply_add_fusion
  3.1 5.4 %collective-permute-start.4 = (s32[4,32]{1,0:T(4,128)S(1)}, s32[4,32]{1,0:T(4,128)}, u32[]{:S(2)}, u32[]{:S(2)}) collective-permute-start(s32[4,32]{1,0:T(4,128)S(1)} %sub.63), channel_id=1, source_target_pairs={{0,16},{1,17},{2,18},{3,19},{4,20},{5,21},{6,22},{7,23},{8,24},{9,... | collective-permute-start | bytes 1544 | tf_op jit(solution)/shard_map/ppermute | solution.py:32
  9.8 0.8 copy.68
  10.6 0.8 slice_bitcast_fusion.3
  11.6 1.2 fusion
  13.3 3.0 %fusion.20 = bf16[64,8,128]{2,1,0:T(8,128)(2,1)S(1)} fusion(bf16[1,1,64,256,128]{4,3,2,1,0:T(8,128)(2,1)} %param.21, bf16[64,8,256]{2,1,0:T(8,128)(2,1)S(1)} %gather_fusion, pred[64]{0:T(512)(128)(4,1)S(1)} %compare_and_fusion), kind=kOutput, calls=%fused_computation.35 | convolution fusion | flops 33751040 | bytes 4587584 | tf_op jit(solution)/shard_map/fpi,pio->pfo/dot_general | solution.py:115
  16.8 2.0 %collective-permute-start.5 = (bf16[4,32,8,128]{3,2,1,0:T(8,128)(2,1)S(1)}, bf16[4,32,8,128]{3,2,1,0:T(8,128)(2,1)}, u32[]{:S(2)}, u32[]{:S(2)}) collective-permute-start(bf16[4,32,8,128]{3,2,1,0:T(8,128)(2,1)S(1)} %bitcast.128), channel_id=1, source_target_pairs={{0,16},{1,17},{2,18},{3,19},{4,20},{5,21},{6,22},{7,23},{8,24},{9,... | collective-permute-start | bytes 786440 | tf_op jit(solution)/shard_map/ppermute | solution.py:32
  19.1 4.9 %all-to-all-start = ((s32[4,1,32]{2,1,0:T(1,128)}), s32[4,1,32]{2,1,0:T(1,128)S(1)}, u32[]{:S(2)}, u32[]{:S(2)}) async-start(s32[4,1,32]{2,1,0:T(1,128)} %bitcast.15), calls=%async_computation | async-start | bytes 4096 | tf_op jit(solution)/shard_map/all_to_all | solution.py:136
  24.0 2.5 %copy_bitcast_fusion = (f32[32,16,512]{2,0,1:T(8,128)}, f32[32,16,512]{2,0,1:T(8,128)}) fusion(f32[1,1,32,16,512]{4,3,2,1,0:T(8,128)S(1)} %get-tuple-element.19, f32[1,1,32,16,512]{4,3,2,1,0:T(8,128)S(1)} %get-tuple-element.20), kind=kLoop, calls=%fused_computation.50 | loop fusion | bytes 4194304 | tf_op jit(solution)/shard_map/squeeze | solution.py:86
  26.6 3.0 %all-to-all-done = s32[4,1,32]{2,1,0:T(1,128)S(1)} async-done(((s32[4,1,32]{2,1,0:T(1,128)}), s32[4,1,32]{2,1,0:T(1,128)S(1)}, u32[]{:S(2)}, u32[]{:S(2)}) %all-to-all-start) | async-done | bytes 544 | tf_op jit(solution)/shard_map/all_to_all | solution.py:136
  30.1 4.0 %all-to-all-start.1 = ((bf16[4,32,8,128]{3,2,1,0:T(8,128)(2,1)}), bf16[4,32,8,128]{3,2,1,0:T(8,128)(2,1)}, u32[]{:S(2)}, u32[]{:S(2)}) async-start(bf16[4,32,8,128]{3,2,1,0:T(8,128)(2,1)} %collective-permute-done.5), calls=%async_computation.1 | async-start | bytes 524288 | tf_op jit(solution)/shard_map/all_to_all | solution.py:135
  34.3 1.6 %copy.99 = f32[1,1,32,16,512]{4,2,3,1,0:T(8,128)} copy(f32[1,1,32,16,512]{4,3,2,1,0:T(8,128)S(1)} %get-tuple-element.21) | data formatting | bytes 2097152
  35.9 6.3 %concatenate.10 = f32[98,16,512]{2,0,1:T(8,128)S(1)} concatenate(f32[32,16,512]{2,0,1:T(8,128)} %bitcast.115, f32[32,16,512]{2,0,1:T(8,128)} %get-tuple-element.26, f32[32,16,512]{2,0,1:T(8,128)} %get-tuple-element.25, f32[1,16,512]{2,0,1:T(1,128)S(1)} %copy.44, f32[1,16,512]{2,0,1:T(1,128)S(1)} %copy_convert_fusion), dimensions={0} | concatenate | bytes 6422528 | tf_op jit(solution)/shard_map/concatenate | solution.py:41
  42.3 1.4 %copy.46 = f32[98,4,512]{2,1,0:T(4,128)} copy(f32[98,4,512]{2,0,1:T(8,128)S(1)} %get-tuple-element.15) | data formatting | bytes 1605632 | tf_op jit(solution)/shard_map/slice | solution.py:16
  43.7 1.3 %collective-permute-start.1 = (f32[98,4,512]{2,1,0:T(4,128)}, f32[98,4,512]{2,1,0:T(4,128)}, u32[]{:S(2)}, u32[]{:S(2)}) collective-permute-start(f32[98,4,512]{2,1,0:T(4,128)} %copy.46), channel_id=1, source_target_pairs={{4,0},{8,4},{12,8},{5,1},{9,5},{13,9},{6,2},{10,6},{14,10},{7,3},{... | collective-permute-start | bytes 2408456 | tf_op jit(solution)/shard_map/ppermute | solution.py:22
  45.0 1.4 %copy.45 = f32[98,4,512]{2,1,0:T(4,128)} copy(f32[98,4,512]{2,0,1:T(8,128)S(1)} %get-tuple-element.14) | data formatting | bytes 1605632 | tf_op jit(solution)/shard_map/slice | solution.py:17
  46.4 5.4 %collective-permute-start = (f32[98,4,512]{2,1,0:T(4,128)}, f32[98,4,512]{2,1,0:T(4,128)}, u32[]{:S(2)}, u32[]{:S(2)}) collective-permute-start(f32[98,4,512]{2,1,0:T(4,128)} %copy.45), channel_id=1, source_target_pairs={{0,4},{4,8},{8,12},{1,5},{5,9},{9,13},{2,6},{6,10},{10,14},{3,7},{... | collective-permute-start | bytes 2408456 | tf_op jit(solution)/shard_map/ppermute | solution.py:20
  53.1 0.7 reduce.3
  53.8 1.7 %copy.100 = bf16[16,8,8,128]{3,1,2,0:T(8,128)(2,1)} copy(bf16[16,8,8,128]{3,2,1,0:T(8,128)(2,1)} %bitcast.59) | data formatting | bytes 524288
  55.5 1.8 %copy.54 = bf16[128,1024]{0,1:T(8,128)(2,1)} copy(bf16[128,1024]{1,0:T(8,128)(2,1)} %bitcast.117) | data formatting | bytes 524288 | tf_op jit(solution)/shard_map/reshape | solution.py:141
  57.4 1.2 convolution_bitcast_fusion
  58.5 1.2 fusion.34
  59.7 1.0 convolution_convert_fusion.1
  60.7 9.6 %all_to_all.19 = bf16[4,32,128]{2,1,0:T(8,128)(2,1)S(1)} all-to-all(bf16[4,32,128]{2,1,0:T(8,128)(2,1)S(1)} %bitcast.129), channel_id=1, replica_groups=mesh['sec'=2,'gx'=4,'gy'=4] {'gx'}, dimensions={0} | all-to-all | bytes 65536 | tf_op jit(solution)/shard_map/all_to_all | solution.py:157
  70.3 1.3 %collective-permute-start.6 = (bf16[4,32,128]{2,1,0:T(8,128)(2,1)S(1)}, bf16[4,32,128]{2,1,0:T(8,128)(2,1)}, u32[]{:S(2)}, u32[]{:S(2)}) collective-permute-start(bf16[4,32,128]{2,1,0:T(8,128)(2,1)S(1)} %all_to_all.19), channel_id=1, source_target_pairs={{16,0},{17,1},{18,2},{19,3},{20,4},{21,5},{22,6},{23,7},{24,8},{25... | collective-permute-start | bytes 98312 | tf_op jit(solution)/shard_map/ppermute | solution.py:32
  71.6 4.6 %collective-permute-done.6 = bf16[4,32,128]{2,1,0:T(8,128)(2,1)} collective-permute-done((bf16[4,32,128]{2,1,0:T(8,128)(2,1)S(1)}, bf16[4,32,128]{2,1,0:T(8,128)(2,1)}, u32[]{:S(2)}, u32[]{:S(2)}) %collective-permute-start.6) | collective-permute-done | bytes 32800 | tf_op jit(solution)/shard_map/ppermute | solution.py:32
  76.2 0.9 fusion.23
  77.2 3.4 %fusion.1 = f32[64,1,256]{2,1,0:T(1,128)S(1)} fusion(bf16[1,1,64,256,128]{4,3,2,1,0:T(8,128)(2,1)} %param.21, bf16[64,128,1]{1,0,2:T(8,128)(2,1)S(1)} %fusion.23), kind=kOutput, calls=%fused_computation.4 | convolution fusion | flops 4194304 | bytes 4276224 | tf_op jit(solution)/shard_map/pio,po->pi/dot_general | solution.py:164
  80.6 0.8 fusion.50
  81.3 0.8 reshape.124
  82.1 1.4 %copy.48 = f32[98,4,512]{2,0,1:T(8,128)S(1)} copy(f32[98,4,512]{2,1,0:T(4,128)} %collective-permute-done.1) | data formatting | bytes 1605632 | tf_op jit(solution)/shard_map/ppermute | solution.py:22
  83.6 1.7 %copy.47 = f32[98,4,512]{2,0,1:T(8,128)S(1)} copy(f32[98,4,512]{2,1,0:T(4,128)} %collective-permute-done) | data formatting | bytes 1605632 | tf_op jit(solution)/shard_map/ppermute | solution.py:20
  85.3 1.9 %pad_maximum_fusion.3 = (f32[98,24,4]{2,0,1:T(8,128)}, f32[98,24,4]{2,0,1:T(8,128)}) fusion(f32[98,4,512]{2,0,1:T(8,128)S(1)} %copy.48, f32[98,16,512]{2,0,1:T(8,128)S(1)} %concatenate.10, f32[98,4,512]{2,0,1:T(8,128)S(1)} %copy.47), kind=kLoop, calls=%fused_computation.31 | loop fusion | flops 37632 | bytes 4892160 | tf_op jit(solution)/shard_map/slice | solution.py:17
  87.2 2.4 %copy.49 = f32[98,24,4]{0,1,2:T(8,128)} copy(f32[98,24,4]{2,0,1:T(8,128)} %get-tuple-element.12) | data formatting | bytes 75264 | tf_op jit(solution)/shard_map/slice | solution.py:17
  89.6 2.3 %copy.50 = f32[98,24,4]{0,1,2:T(8,128)} copy(f32[98,24,4]{2,0,1:T(8,128)} %get-tuple-element.13) | data formatting | bytes 75264 | tf_op jit(solution)/shard_map/slice | solution.py:16
  91.9 1.3 %collective-permute-start.3 = (f32[98,24,4]{0,1,2:T(8,128)}, f32[98,24,4]{0,1,2:T(8,128)}, u32[]{:S(2)}, u32[]{:S(2)}) collective-permute-start(f32[98,24,4]{0,1,2:T(8,128)} %copy.50), channel_id=1, source_target_pairs={{1,0},{2,1},{3,2},{5,4},{6,5},{7,6},{9,8},{10,9},{11,10},{13,12},{... | collective-permute-start | bytes 112904 | tf_op jit(solution)/shard_map/ppermute | solution.py:22
  93.2 3.7 %collective-permute-start.2 = (f32[98,24,4]{0,1,2:T(8,128)}, f32[98,24,4]{0,1,2:T(8,128)}, u32[]{:S(2)}, u32[]{:S(2)}) collective-permute-start(f32[98,24,4]{0,1,2:T(8,128)} %copy.49), channel_id=1, source_target_pairs={{0,1},{1,2},{2,3},{4,5},{5,6},{6,7},{8,9},{9,10},{10,11},{12,13},{... | collective-permute-start | bytes 112904 | tf_op jit(solution)/shard_map/ppermute | solution.py:20
  97.6 2.3 %copy.51 = f32[98,24,4]{2,0,1:T(8,128)} copy(f32[98,24,4]{0,1,2:T(8,128)} %collective-permute-done.2) | data formatting | bytes 75264 | tf_op jit(solution)/shard_map/ppermute | solution.py:20
  99.9 2.3 %copy.52 = f32[98,24,4]{2,0,1:T(8,128)} copy(f32[98,24,4]{0,1,2:T(8,128)} %collective-permute-done.3) | data formatting | bytes 75264 | tf_op jit(solution)/shard_map/ppermute | solution.py:22
  102.2 1.6 %pad_maximum_fusion.4 = (f32[1,24,520]{2,0,1:T(1,128)S(1)}, f32[1,24,520]{2,0,1:T(1,128)S(1)}) fusion(f32[98,24,4]{2,0,1:T(8,128)} %copy.52, f32[98,24,4]{2,0,1:T(8,128)} %copy.51, f32[98,4,512]{2,0,1:T(8,128)} %copy-done.1, f32[98,16,512]{2,0,1:T(8,128)S(1)} %concatenate.10, f32[98,4,512]{2,0,1:T(8,128)} %copy-done.3), kind=kLoop, calls=%fused_computation.76 | loop fusion | flops 99840 | bytes 4992000 | tf_op jit(solution)/shard_map/slice | solution.py:49
  104.3 6.1 %pad_maximum_fusion = f32[98,24,520]{2,0,1:T(8,128)S(1)} fusion(f32[98,24,4]{2,0,1:T(8,128)} %copy.52, f32[98,4,512]{2,0,1:T(8,128)S(1)} %copy-done.2, f32[98,16,512]{2,0,1:T(8,128)S(1)} %concatenate.10, f32[98,4,512]{2,0,1:T(8,128)S(1)} %copy-done.4, f32[98,24,4]{2,0,1:T(8,128)S(1)} %copy-done.5), kind=kLoop, calls=%fused_computation.3 | loop fusion | flops 4892160 | bytes 9784320 | tf_op jit(solution)/shard_map/concatenate | solution.py:18
  110.8 5.0 %bitcast_add_fusion = f32[32,22,518]{2,0,1:T(8,128)S(1)} fusion(f32[98,24,520]{2,0,1:T(8,128)S(1)} %pad_maximum_fusion, f32[22,518]{1,0:T(8,128)S(1)} %slice.176, f32[1,32,32]{2,1,0:T(8,128)S(1)} %copy-done), kind=kOutput, calls=%fused_computation.14 | convolution fusion | flops 144045440 | bytes 19620352 | tf_op jit(solution)/shard_map/lm,mxy->lxy/dot_general | solution.py:36
  115.8 2.2 %fusion.13 = (f32[32,20,516]{2,0,1:T(8,128)S(1)}, f32[32,20,516]{2,0,1:T(8,128)S(1)}) fusion(f32[32,22,518]{2,0,1:T(8,128)S(1)} %bitcast_add_fusion, f32[98,24,520]{2,0,1:T(8,128)S(1)} %pad_maximum_fusion, f32[20,516]{1,0:T(8,128)S(1)} %slice.183), kind=kLoop, calls=%fused_computation.22 | loop fusion | flops 2641920 | bytes 10608960 | tf_op jit(solution)/shard_map/mul | solution.py:59
  118.1 3.6 %bitcast_add_fusion.1 = f32[32,18,514]{2,0,1:T(8,128)S(1)} fusion(f32[32,20,516]{2,0,1:T(8,128)S(1)} %get-tuple-element.9, f32[32,20,516]{2,0,1:T(8,128)S(1)} %get-tuple-element.8, f32[32,22,518]{2,0,1:T(8,128)S(1)} %bitcast_add_fusion, f32[18,514]{1,0:T(8,128)S(1)} %slice.182, f32[1,32,32]{2,1,0:T(8,128)S(1)} %copy-done), kind=kOutput, calls=%fused_computation.28 | convolution fusion | flops 116945280 | bytes 16069120 | tf_op jit(solution)/shard_map/lm,mxy->lxy/dot_general | solution.py:36
  121.7 1.7 %fusion.31 = (f32[1,32,16,512]{3,1,2,0:T(8,128)S(1)}, f32[1,32,16,512]{3,1,2,0:T(8,128)S(1)}, f32[1,32,16,512]{3,1,2,0:T(8,128)S(1)}) fusion(f32[32,18,514]{2,0,1:T(8,128)S(1)} %bitcast_add_fusion.1, f32[32,20,516]{2,0,1:T(8,128)S(1)} %get-tuple-element.8, f32[16,512]{1,0:T(8,128)S(1)} %slice.195, f32[32,20,516]{2,0,1:T(8,128)S(1)} %get-tuple-element.9), kind=kLoop, calls=%fused_computation.48 | loop fusion | flops 2097152 | bytes 10518528 | tf_op jit(solution)/shard_map/stack | solution.py:93
  123.8 3.5 %copy.56 = f32[1,3,32,16,512]{4,3,2,1,0:T(8,128)} copy(f32[1,3,32,16,512]{4,2,3,1,0:T(8,128)S(1)} %maximum_bitcast_fusion) | data formatting | bytes 6291456
  (65 shorter events, 6.9 us)
Async XLA Ops:
  0.6 110.2 %copy-start = (f32[1,32,32]{2,1,0:T(8,128)S(1)}, f32[1,32,32]{2,1,0:T(8,128)}, u32[]{:S(2)}) copy-start(f32[1,32,32]{2,1,0:T(8,128)} %param.14) | copy-start | bytes 12292
  2.9 13.5 %copy-start.14 = (s32[64]{0:T(128)}, s32[64]{0:T(128)S(1)}, u32[]{:S(2)}) copy-start(s32[64]{0:T(128)S(1)} %multiply_add_fusion) | copy-start | bytes 772
  3.1 16.0 %collective-permute-start.4 = (s32[4,32]{1,0:T(4,128)S(1)}, s32[4,32]{1,0:T(4,128)}, u32[]{:S(2)}, u32[]{:S(2)}) collective-permute-start(s32[4,32]{1,0:T(4,128)S(1)} %sub.63), channel_id=1, source_target_pairs={{0,16},{1,17},{2,18},{3,19},{4,20},{5,21},{6,22},{7,23},{8,24},{9,... | collective-permute-start | bytes 1544 | tf_op jit(solution)/shard_map/ppermute | solution.py:32
  13.3 5.5 %copy-start.6 = (f32[1,3,32,16,512]{4,3,2,1,0:T(8,128)S(1)}, f32[1,3,32,16,512]{4,3,2,1,0:T(8,128)}, u32[]{:S(2)}) copy-start(f32[1,3,32,16,512]{4,3,2,1,0:T(8,128)} %param.11) | copy-start | bytes 9437188
  16.8 12.8 %collective-permute-start.5 = (bf16[4,32,8,128]{3,2,1,0:T(8,128)(2,1)S(1)}, bf16[4,32,8,128]{3,2,1,0:T(8,128)(2,1)}, u32[]{:S(2)}, u32[]{:S(2)}) collective-permute-start(bf16[4,32,8,128]{3,2,1,0:T(8,128)(2,1)S(1)} %bitcast.128), channel_id=1, source_target_pairs={{0,16},{1,17},{2,18},{3,19},{4,20},{5,21},{6,22},{7,23},{8,24},{9,... | collective-permute-start | bytes 786440 | tf_op jit(solution)/shard_map/ppermute | solution.py:32
  19.1 10.4 %all-to-all-start = ((s32[4,1,32]{2,1,0:T(1,128)}), s32[4,1,32]{2,1,0:T(1,128)S(1)}, u32[]{:S(2)}, u32[]{:S(2)}) async-start(s32[4,1,32]{2,1,0:T(1,128)} %bitcast.15), calls=%async_computation | async-start | bytes 4096 | tf_op jit(solution)/shard_map/all_to_all | solution.py:136
  24.0 10.2 %copy-start.8 = (s32[1,16,512]{2,1,0:T(8,128)S(1)}, s32[1,16,512]{2,1,0:T(8,128)}, u32[]{:S(2)}) copy-start(s32[1,16,512]{2,1,0:T(8,128)} %param.13) | copy-start | bytes 98308
  24.0 10.2 %copy-start.9 = (f32[1,16,512]{2,1,0:T(8,128)S(1)}, f32[1,16,512]{2,1,0:T(8,128)}, u32[]{:S(2)}) copy-start(f32[1,16,512]{2,1,0:T(8,128)} %param.12) | copy-start | bytes 98308
  29.6 0.6 copy-start.10
  30.1 23.7 %all-to-all-start.1 = ((bf16[4,32,8,128]{3,2,1,0:T(8,128)(2,1)}), bf16[4,32,8,128]{3,2,1,0:T(8,128)(2,1)}, u32[]{:S(2)}, u32[]{:S(2)}) async-start(bf16[4,32,8,128]{3,2,1,0:T(8,128)(2,1)} %collective-permute-done.5), calls=%async_computation.1 | async-start | bytes 524288 | tf_op jit(solution)/shard_map/all_to_all | solution.py:135
  42.3 9.6 %copy-start.7 = (f32[1,16,512]{2,1,0:T(8,128)S(1)}, f32[1,16,512]{2,1,0:T(8,128)}, u32[]{:S(2)}) copy-start(f32[1,16,512]{2,1,0:T(8,128)} %param.15) | copy-start | bytes 98308
  42.3 10.7 %copy-start.11 = (s32[4,1,32]{2,1,0:T(1,128)S(1)}, s32[4,1,32]{2,1,0:T(1,128)}, u32[]{:S(2)}) copy-start(s32[4,1,32]{2,1,0:T(1,128)} %copy-done.10) | copy-start | bytes 1540
  43.7 38.4 %collective-permute-start.1 = (f32[98,4,512]{2,1,0:T(4,128)}, f32[98,4,512]{2,1,0:T(4,128)}, u32[]{:S(2)}, u32[]{:S(2)}) collective-permute-start(f32[98,4,512]{2,1,0:T(4,128)} %copy.46), channel_id=1, source_target_pairs={{4,0},{8,4},{12,8},{5,1},{9,5},{13,9},{6,2},{10,6},{14,10},{7,3},{... | collective-permute-start | bytes 2408456 | tf_op jit(solution)/shard_map/ppermute | solution.py:22
  46.4 37.1 %collective-permute-start = (f32[98,4,512]{2,1,0:T(4,128)}, f32[98,4,512]{2,1,0:T(4,128)}, u32[]{:S(2)}, u32[]{:S(2)}) collective-permute-start(f32[98,4,512]{2,1,0:T(4,128)} %copy.45), channel_id=1, source_target_pairs={{0,4},{4,8},{8,12},{1,5},{5,9},{9,13},{2,6},{6,10},{10,14},{3,7},{... | collective-permute-start | bytes 2408456 | tf_op jit(solution)/shard_map/ppermute | solution.py:20
  53.8 3.5 %copy-start.12 = (s32[128]{0:T(128)}, s32[128]{0:T(128)S(1)}, u32[]{:S(2)}) copy-start(s32[128]{0:T(128)S(1)} %eq.71) | copy-start | bytes 1540
  70.3 5.9 %collective-permute-start.6 = (bf16[4,32,128]{2,1,0:T(8,128)(2,1)S(1)}, bf16[4,32,128]{2,1,0:T(8,128)(2,1)}, u32[]{:S(2)}, u32[]{:S(2)}) collective-permute-start(bf16[4,32,128]{2,1,0:T(8,128)(2,1)S(1)} %all_to_all.19), channel_id=1, source_target_pairs={{16,0},{17,1},{18,2},{19,3},{20,4},{21,5},{22,6},{23,7},{24,8},{25... | collective-permute-start | bytes 98312 | tf_op jit(solution)/shard_map/ppermute | solution.py:32
  77.2 3.4 %copy-start.13 = (s32[1,1,64]{2,1,0:T(1,128)S(1)}, s32[1,1,64]{2,1,0:T(1,128)}, u32[]{:S(2)}) copy-start(s32[1,1,64]{2,1,0:T(1,128)} %param.19) | copy-start | bytes 772
  83.5 3.7 %copy-start.1 = (f32[98,4,512]{2,0,1:T(8,128)}, f32[98,4,512]{2,0,1:T(8,128)S(1)}, u32[]{:S(2)}) copy-start(f32[98,4,512]{2,0,1:T(8,128)S(1)} %copy.48) | copy-start | bytes 2408452
  85.3 1.9 %copy-start.3 = (f32[98,4,512]{2,0,1:T(8,128)}, f32[98,4,512]{2,0,1:T(8,128)S(1)}, u32[]{:S(2)}) copy-start(f32[98,4,512]{2,0,1:T(8,128)S(1)} %copy.47) | copy-start | bytes 2408452
  91.9 8.0 %collective-permute-start.3 = (f32[98,24,4]{0,1,2:T(8,128)}, f32[98,24,4]{0,1,2:T(8,128)}, u32[]{:S(2)}, u32[]{:S(2)}) collective-permute-start(f32[98,24,4]{0,1,2:T(8,128)} %copy.50), channel_id=1, source_target_pairs={{1,0},{2,1},{3,2},{5,4},{6,5},{7,6},{9,8},{10,9},{11,10},{13,12},{... | collective-permute-start | bytes 112904 | tf_op jit(solution)/shard_map/ppermute | solution.py:22
  93.2 4.4 %collective-permute-start.2 = (f32[98,24,4]{0,1,2:T(8,128)}, f32[98,24,4]{0,1,2:T(8,128)}, u32[]{:S(2)}, u32[]{:S(2)}) collective-permute-start(f32[98,24,4]{0,1,2:T(8,128)} %copy.49), channel_id=1, source_target_pairs={{0,1},{1,2},{2,3},{4,5},{5,6},{6,7},{8,9},{9,10},{10,11},{12,13},{... | collective-permute-start | bytes 112904 | tf_op jit(solution)/shard_map/ppermute | solution.py:20
  102.2 1.7 %copy-start.2 = (f32[98,4,512]{2,0,1:T(8,128)S(1)}, f32[98,4,512]{2,0,1:T(8,128)}, u32[]{:S(2)}) copy-start(f32[98,4,512]{2,0,1:T(8,128)} %copy-done.1) | copy-start | bytes 2408452
  102.2 1.7 %copy-start.4 = (f32[98,4,512]{2,0,1:T(8,128)S(1)}, f32[98,4,512]{2,0,1:T(8,128)}, u32[]{:S(2)}) copy-start(f32[98,4,512]{2,0,1:T(8,128)} %copy-done.3) | copy-start | bytes 2408452
  102.2 2.1 %copy-start.5 = (f32[98,24,4]{2,0,1:T(8,128)S(1)}, f32[98,24,4]{2,0,1:T(8,128)}, u32[]{:S(2)}) copy-start(f32[98,24,4]{2,0,1:T(8,128)} %copy.51) | copy-start | bytes 112900
where the time goes:
time: 130 us; the launch traced here: 127 us
  local copies, waits for them, and re-layouts  39.7 us (31%)
  starting transfers between devices  29.3 us (23%)
  matrix products  21.6 us (17%)
  other arithmetic  18.5 us (14%)
  blocking collectives  9.65 us (7%)
  waiting for transfers between devices  7.62 us (6%)
    unnamed x43, local copies, waits for them, and re-layouts  10.3 us
    all_to_all x1, blocking collectives, local(): lax.all_to_all(returning, 'gx', split_axis=0, concat_axis=0, tiled=True)  9.65 us
    ppermute x2, starting transfers between devices, extended(): lax.ppermute(tail, axis, [(i, (i + 1) % count) for i in range(ends)])  9.09 us
    ppermute x3, starting transfers between devices, shifted_2(): return lax.ppermute(value, axis, pairs)  8.72 us
    dot_general x2, matrix products, vertical_mix(): jnp.einsum('lm,mxy->lxy', matrix, right_side, precision=HIGHEST_PRECISION)  8.64 us
    concatenate x1, local copies, waits for them, and re-layouts, substeps_deep(): jnp.concatenate([pressure, eastward, northward, sound_speed[None], wetnes...  6.27 us
    concatenate x1, other arithmetic, extended(): jnp.concatenate([lax.ppermute(tail, axis, [(i, (i + 1) % count) for i in...  6.13 us
    all_to_all x1, starting transfers between devices, local(): lax.all_to_all(shifted[1], 'gx', split_axis=0, concat_axis=0, tiled=True)  4.88 us
  transfers between devices with their start and end apart: 9, of which 2 were waited for; matrix products, arithmetic and copies ran while one was open for 32% of the time, Pallas kernels for 0%

commit v1 on v0

v1 whole, which is shorter than its diff:
```python
import functools

import jax
import jax.numpy as jnp
from jax import lax
from jax.experimental import pallas as pl
from jax.experimental.pallas import tpu as pltpu
from jax.sharding import PartitionSpec as P

MESH = pl.DeviceIdType.MESH
F32 = jnp.float32
BF16 = jnp.bfloat16
LANES = 128
CHUNKS = 8


def iota(shape, axis):
    return lax.broadcasted_iota(jnp.int32, shape, axis)


def split(value, parts):
    pieces = []
    for _ in range(parts):
        piece = value.astype(BF16)
        pieces.append(piece)
        value = value - piece.astype(F32)
    return pieces


def dot(a, b):
    return jnp.dot(a, b, preferred_element_type=F32)


def block_key(index, rows, per_row):
    return (index & (rows - 1)) * per_row + (index >> (rows.bit_length() - 1))


def kernel(
    n_gx,
    n_gy,
    state,
    speed,
    mask,
    vertical,
    temp,
    coef,
    gain,
    tile_in,
    source_in,
    target_in,
    source_s,
    weights,
    final,
    surface,
    raw,
    out,
    wbuf,
    u0,
    p1,
    u1,
    v1,
    p2,
    colsend,
    colrecv,
    ybuf,
    yrecv,
    trecv,
    xbuf,
    load_sem,
    w_sem,
    row_send,
    row_recv,
    col_send,
    col_recv,
    y_send,
    y_recv,
    t_send,
    t_recv,
    x_send,
    x_recv,
    out_sem,
):
    sec = lax.axis_index("sec")
    a = lax.axis_index("gx")
    b = lax.axis_index("gy")
    levels, rows, width = state.shape[2:]
    tiles = width // LANES
    pairs, in_width, out_width = wbuf.shape
    in_per_row = width // in_width
    out_per_row = width // out_width
    in_blocks = rows * in_per_row
    out_blocks = rows * out_per_row
    per_chunk = pairs // CHUNKS

    def load(f, i):
        part = state.at[0, f, :, :, pl.ds(i * LANES, LANES)]
        return pltpu.make_async_copy(part, raw.at[f, i], load_sem.at[f, i])

    def load_weights(i):
        part = pl.ds(i * per_chunk, per_chunk)
        return pltpu.make_async_copy(weights.at[0, 0, part], wbuf.at[part], w_sem.at[i])

    for f in (1, 2, 0):
        for i in range(tiles):
            load(f, i).start()
    for i in range(CHUNKS):
        load_weights(i).start()

    barrier = pltpu.get_barrier_semaphore()
    for s in range(2):
        for t in range(n_gx):

            @pl.when(jnp.logical_or(s != sec, t != a))
            def _():
                pl.semaphore_signal(barrier, inc=1, device_id=(s, t, b), device_id_type=MESH)

    @pl.when(b > 0)
    def _():
        pl.semaphore_signal(barrier, inc=1, device_id=(sec, a, b - 1), device_id_type=MESH)

    @pl.when(b < n_gy - 1)
    def _():
        pl.semaphore_signal(barrier, inc=1, device_id=(sec, a, b + 1), device_id_type=MESH)

    beside = (b > 0).astype(jnp.int32) + (b < n_gy - 1).astype(jnp.int32)

    @pl.when(a == 0)
    def _():
        for buf in (u0, p1, u1, p2):
            buf[0] = jnp.zeros((levels, width), F32)

    @pl.when(a == n_gx - 1)
    def _():
        for buf in (u0, p1, u1, p2):
            buf[rows + 1] = jnp.zeros((levels, width), F32)

    @pl.when(b == 0)
    def _():
        for stage in range(4):
            colrecv[stage, 0] = jnp.zeros((levels, LANES), F32)

    @pl.when(b == n_gy - 1)
    def _():
        for stage in range(4):
            colrecv[stage, 1] = jnp.zeros((levels, LANES), F32)

    def row_copy(stage, buf, side):
        src, dst = (1, rows + 1) if side == 0 else (rows, 0)
        return pltpu.make_async_remote_copy(
            src_ref=buf.at[src],
            dst_ref=buf.at[dst],
            send_sem=row_send.at[stage, side],
            recv_sem=row_recv.at[stage, side],
            device_id=(sec, a - 1 if side == 0 else a + 1, b),
            device_id_type=MESH,
        )

    def col_copy(stage, side):
        return pltpu.make_async_remote_copy(
            src_ref=colsend.at[stage, side],
            dst_ref=colrecv.at[stage, 1 - side],
            send_sem=col_send.at[stage, side],
            recv_sem=col_recv.at[stage, side],
            device_id=(sec, a, b - 1 if side == 0 else b + 1),
            device_id_type=MESH,
        )

    row_ok = (a > 0, a < n_gx - 1)
    col_ok = (b > 0, b < n_gy - 1)

    def send_rows(stage, buf):
        for side in range(2):

            @pl.when(row_ok[side])
            def _(side=side):
                row_copy(stage, buf, side).start()

    def send_cols(stage):
        for side in range(2):

            @pl.when(col_ok[side])
            def _(side=side):
                col_copy(stage, side).start()

    def wait_halo(stage, buf):
        for side in range(2):

            @pl.when(col_ok[side])
            def _(side=side):
                col_copy(stage, 1 - side).wait_recv()

        for side in range(2):

            @pl.when(row_ok[side])
            def _(side=side):
                row_copy(stage, buf, 1 - side).wait_recv()

    def wait_sent(stage, buf):
        for side in range(2):

            @pl.when(col_ok[side])
            def _(side=side):
                col_copy(stage, side).wait_send()

            @pl.when(row_ok[side])
            def _(side=side):
                row_copy(stage, buf, side).wait_send()

    lane = iota((levels, LANES), 1)

    def flat(buf, f):
        return [buf.at[f, i].reshape(levels * rows, LANES) for i in range(tiles)]

    flat_raw = [flat(raw, f) for f in range(3)]
    flat_out = [flat(out, f) for f in range(3)]

    def column(f, x):
        parts = [ref[pl.ds(x, levels, stride=rows), :] for ref in flat_raw[f]]
        return jnp.concatenate(parts, axis=1)

    def put(f, x, value):
        for i, ref in enumerate(flat_out[f]):
            ref[pl.ds(x, levels, stride=rows), :] = value[:, i * LANES : (i + 1) * LANES]

    def loaded(f):
        for i in range(tiles):
            load(f, i).wait()

    def pack(value, x, carry):
        low, high = carry
        low = jnp.where(lane == x, pltpu.roll(value[:, :LANES], x, 1), low)
        high = jnp.where(lane == x, pltpu.roll(value[:, width - LANES :], x + 1, 1), high)
        return low, high

    def along_y(value, stage, x):
        left = pltpu.roll(colrecv[stage, 0], lax.rem(LANES - x, LANES), 1)
        right = pltpu.roll(colrecv[stage, 1], LANES - 1 - x, 1)
        plus = pltpu.roll(value, width - 1, 1)
        minus = pltpu.roll(value, 1, 1)
        end = jnp.where(lane == LANES - 1, right, plus[:, width - LANES :])
        start = jnp.where(lane == 0, left, minus[:, :LANES])
        plus = jnp.concatenate([plus[:, : width - LANES], end], axis=1)
        minus = jnp.concatenate([start, minus[:, LANES:]], axis=1)
        return plus - minus

    m_high, m_low = split(vertical[0], 2)
    m_high, m_low = m_high.astype(F32), m_low.astype(F32)
    mixer = jnp.concatenate([m_high, m_high, m_low, m_low], axis=1).astype(BF16)

    def mix(right_side):
        high, low = split(right_side, 2)
        return right_side + dot(mixer, jnp.concatenate([high, low, high, low], axis=0))

    def pressure_row(stage, x, p, u_buf, v):
        divergence = (u_buf[x + 2] - u_buf[x]) + along_y(v, stage, x)
        return mix(p - speed[0, pl.ds(x, 1), :] * divergence)

    def sweep(row, after_edges, carry):
        carry = lax.fori_loop(0, 2, lambda i, c: row(i * (rows - 1), c), carry)
        after_edges()
        carry = lax.fori_loop(
            0, (rows - 2) // 2, lambda i, c: row(2 * i + 2, row(2 * i + 1, c)), carry
        )
        return carry

    blank = jnp.zeros((levels, LANES), F32)
    pair = (blank, blank)

    def start_cols(stage, carry):
        colsend[stage, 0] = carry[0]
        colsend[stage, 1] = carry[1]
        send_cols(stage)

    loaded(1)
    u0[1] = column(1, 0)
    u0[rows] = column(1, rows - 1)
    pl.semaphore_wait(barrier, 2 * n_gx - 1 + beside)
    send_rows(0, u0)
    loaded(2)
    start_cols(0, lax.fori_loop(0, rows, lambda x, c: pack(column(2, x), x, c), pair))
    loaded(0)

    def wide_row(value):
        return value[0, 0].reshape(1, pairs).astype(F32)

    diagonal = iota((pairs, pairs), 0) == iota((pairs, pairs), 1)

    def upright(row):
        return jnp.sum(jnp.where(diagonal, row, 0.0), axis=1, keepdims=True)

    slots = n_gx * out_blocks
    shift = out_blocks.bit_length() - 1

    def slot_key(index):
        within = block_key(index & (out_blocks - 1), rows, out_per_row)
        return ((index >> shift) * out_blocks + within).astype(F32)

    tile_col = tile_in[0, 0].astype(F32)
    target_row = wide_row(target_in)

    def y_copy(t):
        return pltpu.make_async_remote_copy(
            src_ref=ybuf.at[t],
            dst_ref=yrecv.at[a],
            send_sem=y_send.at[t],
            recv_sem=y_recv.at[a],
            device_id=(1, t, b),
            device_id_type=MESH,
        )

    def x_copy():
        return pltpu.make_async_remote_copy(
            src_ref=xbuf,
            dst_ref=xbuf,
            send_sem=x_send,
            recv_sem=x_recv,
            device_id=(0, a, b),
            device_id_type=MESH,
        )

    def t_copy(t):
        return pltpu.make_async_remote_copy(
            src_ref=trecv.at[a],
            dst_ref=trecv.at[a],
            send_sem=t_send.at[t],
            recv_sem=t_recv.at[a],
            device_id=(1, t, b),
            device_id_type=MESH,
        )

    def wide(j):
        return jnp.concatenate([wbuf[j], wbuf[j + 1]], axis=1)

    @pl.when(sec == 0)
    def _():
        drivers = [
            jnp.concatenate([raw[f, i, 0] for i in range(tiles)], axis=1) for f in range(3)
        ] + [temp[0]]
        heat = jnp.zeros((rows, width), F32)
        for f in range(coef.shape[0]):
            total = coef[f, 0] * drivers[0]
            for k in range(1, 4):
                total = total + coef[f, k] * drivers[k]
            heat = heat + gain[f] * jnp.tanh(total).astype(BF16).astype(F32)
        blocks = jnp.concatenate(
            [heat[:, i * in_width : (i + 1) * in_width] for i in range(in_per_row)], axis=0
        )
        source_col = upright(wide_row(source_in))
        key = block_key(iota((pairs, in_blocks), 1), rows, in_per_row).astype(F32)
        picking = (source_col == key).astype(F32).astype(BF16)
        high, low = [dot(picking, piece) for piece in split(blocks, 2)]
        sub = iota((8, out_width), 0)
        groups = []
        for g in range(pairs // 8):
            if g % (per_chunk // 8) == 0:
                load_weights(g * 8 // per_chunk).wait()
            part = slice(8 * g, 8 * g + 8)
            left = jnp.concatenate([high[part], low[part]], axis=0).astype(BF16)
            group = jnp.zeros((8, out_width), F32)
            for i in range(0, 8, 2):
                both = dot(left, wide(8 * g + i))
                both = both[:8] + both[8:]
                group = jnp.where(sub == i, both[:, :out_width], group)
                group = jnp.where(sub == i + 1, both[:, out_width:], group)
            groups.append(group)
        heated = jnp.concatenate(groups, axis=0)
        tile_row = jnp.sum(jnp.where(diagonal, tile_col, 0.0), axis=0, keepdims=True)
        slot_row = tile_row * out_blocks + target_row
        placing = (slot_key(iota((slots, pairs), 0)) == slot_row).astype(F32).astype(BF16)
        dense = sum(dot(placing, piece) for piece in split(heated, 3))
        ybuf[...] = dense.reshape(n_gx, out_blocks, out_width)
        for t in range(n_gx):
            y_copy(t).start()

    def fill(x, c):
        u0[x + 1] = column(1, x)
        return c

    lax.fori_loop(1, rows - 1, fill, 0)
    wait_halo(0, u0)

    def first_pressure(x, c):
        p = pressure_row(0, x, column(0, x), u0, column(2, x))
        p1[x + 1] = p
        return pack(p, x, c)

    start_cols(1, sweep(first_pressure, lambda: send_rows(1, p1), pair))
    wait_halo(1, p1)

    def free(x):
        return mask[0, pl.ds(x, 1), :].astype(F32)

    def first_velocity(x, c):
        w = free(x)
        u1[x + 1] = w * (u0[x + 1] - 0.5 * (p1[x + 2] - p1[x]))
        v = w * (column(2, x) - 0.5 * along_y(p1[x + 1], 1, x))
        v1[x] = v
        return pack(v, x, c)

    start_cols(2, sweep(first_velocity, lambda: send_rows(2, u1), pair))

    def as_blocks(value):
        return jnp.concatenate(
            [value[:, i * out_width : (i + 1) * out_width] for i in range(out_per_row)], axis=0
        )

    @pl.when(sec == 1)
    def _():
        heating = jnp.zeros((out_blocks, out_width), F32)
        for t in range(n_gx):
            pltpu.make_async_remote_copy(
                src_ref=ybuf.at[t],
                dst_ref=yrecv.at[t],
                send_sem=y_send.at[t],
                recv_sem=y_recv.at[t],
                device_id=(0, t, b),
                device_id_type=MESH,
            ).wait_recv()
            heating = heating + yrecv[t]
        ocean = as_blocks(temp[0]) + as_blocks(mask[0].astype(F32)) * heating
        trecv[a] = ocean.astype(BF16)
        for t in range(n_gx):

            @pl.when(t != a)
            def _():
                t_copy(t).start()

        surface[0] = jnp.concatenate(
            [ocean[i * rows : (i + 1) * rows] for i in range(out_per_row)], axis=1
        )

    wait_halo(2, u1)

    def second_pressure(x, c):
        p = pressure_row(2, x, p1[x + 1], u1, v1[x])
        p2[x + 1] = p
        put(0, x, p)
        return pack(p, x, c)

    start_cols(3, sweep(second_pressure, lambda: send_rows(3, p2), pair))

    def store(f, i):
        part = final.at[0, f, :, :, pl.ds(i * LANES, LANES)]
        return pltpu.make_async_copy(out.at[f, i], part, out_sem.at[f, i])

    def store_all(f):
        for i in range(tiles):
            store(f, i).start()

    store_all(0)

    @pl.when(sec == 1)
    def _():
        for i in range(CHUNKS):
            load_weights(i).wait()
        for t in range(n_gx):

            @pl.when(t != a)
            def _():
                pltpu.make_async_remote_copy(
                    src_ref=trecv.at[t],
                    dst_ref=trecv.at[t],
                    send_sem=t_send.at[t],
                    recv_sem=t_recv.at[t],
                    device_id=(1, t, b),
                    device_id_type=MESH,
                ).wait_recv()

        slot_col = tile_col * out_blocks + upright(target_row)
        picking = (slot_key(iota((pairs, slots), 1)) == slot_col).astype(F32).astype(BF16)
        returned = dot(picking, trecv[...].reshape(slots, out_width))
        key = block_key(iota((in_blocks, out_width), 0), rows, in_per_row)
        total = jnp.zeros((in_blocks, in_width), F32)
        for j in range(0, pairs, 2):
            left = jnp.concatenate(
                [
                    jnp.where(key == source_s[0, 0, i], returned[i : i + 1], 0.0)
                    for i in (j, j + 1)
                ],
                axis=1,
            ).astype(BF16)
            total = total + lax.dot_general(
                left, wide(j), (((1,), (1,)), ((), ())), preferred_element_type=F32
            )
        xbuf[...] = jnp.concatenate(
            [total[i * rows : (i + 1) * rows] for i in range(in_per_row)], axis=1
        )
        x_copy().start()

    wait_halo(3, p2)

    def second_velocity(x, c):
        w = free(x)
        put(1, x, w * (u1[x + 1] - 0.5 * (p2[x + 2] - p2[x])))
        put(2, x, w * (v1[x] - 0.5 * along_y(p2[x + 1], 3, x)))
        return c

    sweep(second_velocity, lambda: None, 0)
    store_all(1)
    store_all(2)

    for stage, buf in enumerate((u0, p1, u1, p2)):
        wait_sent(stage, buf)

    @pl.when(sec == 0)
    def _():
        for t in range(n_gx):
            y_copy(t).wait_send()
        x_copy().wait_recv()
        surface[0] = xbuf[...]

    @pl.when(sec == 1)
    def _():
        for t in range(n_gx):

            @pl.when(t != a)
            def _():
                t_copy(t).wait_send()

        x_copy().wait_send()

    for f in range(3):
        for i in range(tiles):
            store(f, i).wait()


def local(n_gx, n_gy, *args):
    state, speed, mask, vertical, temp, coef, gain, tile, source, target, weights = args
    _, fields, levels, rows, width = state.shape
    pairs, in_width, out_width = weights.shape[2:]
    out_blocks = rows * width // out_width
    vmem = pl.BlockSpec(memory_space=pltpu.VMEM)
    smem = pl.BlockSpec(memory_space=pltpu.SMEM)
    hbm = pl.BlockSpec(memory_space=pl.ANY)
    dma = pltpu.SemaphoreType.DMA
    tiled = pltpu.VMEM((fields, width // LANES, levels, rows, LANES), F32)
    tall = pltpu.VMEM((rows + 2, levels, width), F32)
    return pl.pallas_call(
        functools.partial(kernel, n_gx, n_gy),
        out_shape=(
            jax.ShapeDtypeStruct(state.shape, F32),
            jax.ShapeDtypeStruct(temp.shape, F32),
        ),
        in_specs=[hbm, vmem, vmem, vmem, vmem, smem, smem, vmem, vmem, vmem, smem, hbm],
        out_specs=(hbm, vmem),
        scratch_shapes=[
            tiled,
            tiled,
            pltpu.VMEM((pairs, in_width, out_width), BF16),
            tall,
            tall,
            tall,
            pltpu.VMEM((rows, levels, width), F32),
            tall,
            pltpu.VMEM((4, 2, levels, LANES), F32),
            pltpu.VMEM((4, 2, levels, LANES), F32),
            pltpu.VMEM((n_gx, out_blocks, out_width), F32),
            pltpu.VMEM((n_gx, out_blocks, out_width), F32),
            pltpu.VMEM((n_gx, out_blocks, out_width), BF16),
            pltpu.VMEM((rows, width), F32),
            dma((fields, width // LANES)),
            dma((CHUNKS,)),
            dma((4, 2)),
            dma((4, 2)),
            dma((4, 2)),
            dma((4, 2)),
            dma((n_gx,)),
            dma((n_gx,)),
            dma((n_gx,)),
            dma((n_gx,)),
            dma(()),
            dma(()),
            dma((fields, width // LANES)),
        ],
        compiler_params=pltpu.CompilerParams(
            collective_id=0, has_side_effects=True, vmem_limit_bytes=40 * 2**20
        ),
    )(state, speed, mask, vertical, temp, coef, gain, tile, source, target, source, weights)


def solution(mesh):
    return jax.shard_map(
        functools.partial(local, mesh.shape["gx"], mesh.shape["gy"]),
        mesh=mesh,
        in_specs=(
            P("sec", None, None, "gx", "gy"),
            P("sec", "gx", "gy"),
            P("sec", "gx", "gy"),
            P("sec", None, None),
            P("sec", "gx", "gy"),
            P(),
            P(),
            P("gx", "gy", None, None),
            P("gx", "gy", None),
            P("gx", "gy", None),
            P("gx", "gy", None, None, None),
        ),
        out_specs=(P("sec", None, None, "gx", "gy"), P("sec", "gx", "gy")),
        check_vma=False,
    )
```

time: 130 us -> 44.2 us (0.34)
  the two profiles are of different devices: /device:TPU:0 before, /device:TPU:1 now
where the time goes in v1:
time: 44.2 us; the launch traced here: 43.7 us
  Pallas kernels  30.2 us (68%)
  local copies, waits for them, and re-layouts  12.8 us (29%)
  between operations  0.65 us (1%)
    pallas_call x1, Pallas kernels, local(): pl.pallas_call(functools.partial(kernel, n_gx, n_gy), out_shape=(jax.Shap...  30.2 us
    unnamed x22, local copies, waits for them, and re-layouts  12.8 us

profile of v1, /device:TPU:1, one launch (start us, length us, event | category | flops | bytes accessed | tf_op | source)
XLA Modules:
  0.0 43.7 jit_solution(11424355460858655920)
XLA Ops:
  0.6 0.8 %copy.13.coef = f32[8,4]{1,0:T(8,128)S(1)} copy(f32[8,4]{0,1:T(4,128)} %param.16) | data formatting | bytes 256 | tf_op args[5]
  1.4 0.7 %copy.14.tile_in = s32[1,1,64,1]{3,2,1,0:T(8,128)S(1)} copy(s32[1,1,64,1]{2,3,1,0:T(1,128)} %param.18) | data formatting | bytes 512 | tf_op args[7]
  2.1 0.0 copy-start
  2.1 2.2 %copy-done = bf16[1,1,64,256,128]{4,3,2,1,0:T(8,128)(2,1)S(1)} copy-done((bf16[1,1,64,256,128]{4,3,2,1,0:T(8,128)(2,1)S(1)}, bf16[1,1,64,256,128]{4,3,2,1,0:T(8,128)(2,1)}, u32[]{:S(2)}) %copy-start) | copy-done | bytes 4194328
  4.3 0.0 copy-start.1
  4.3 1.9 %copy-done.1 = f32[1,3,32,16,512]{4,3,2,1,0:T(8,128)S(1)} copy-done((f32[1,3,32,16,512]{4,3,2,1,0:T(8,128)S(1)}, f32[1,3,32,16,512]{4,3,2,1,0:T(8,128)}, u32[]{:S(2)}) %copy-start.1) | copy-done | bytes 3145752
  6.2 0.0 copy-start.2
  6.2 0.8 %copy-done.2 = f32[1,16,512]{2,1,0:T(8,128)S(1)} copy-done((f32[1,16,512]{2,1,0:T(8,128)S(1)}, f32[1,16,512]{2,1,0:T(8,128)}, u32[]{:S(2)}) %copy-start.2) | copy-done | bytes 32792
  7.0 0.0 copy-start.3
  7.0 0.8 %copy-done.3 = s32[1,16,512]{2,1,0:T(8,128)S(1)} copy-done((s32[1,16,512]{2,1,0:T(8,128)S(1)}, s32[1,16,512]{2,1,0:T(8,128)}, u32[]{:S(2)}) %copy-start.3) | copy-done | bytes 32792
  7.7 0.0 copy-start.4
  7.7 0.8 %copy-done.4 = f32[1,16,512]{2,1,0:T(8,128)S(1)} copy-done((f32[1,16,512]{2,1,0:T(8,128)S(1)}, f32[1,16,512]{2,1,0:T(8,128)}, u32[]{:S(2)}) %copy-start.4) | copy-done | bytes 32792
  8.5 0.0 copy-start.5
  8.5 0.7 %copy-done.5 = f32[1,32,32]{2,1,0:T(8,128)S(1)} copy-done((f32[1,32,32]{2,1,0:T(8,128)S(1)}, f32[1,32,32]{2,1,0:T(8,128)}, u32[]{:S(2)}) %copy-start.5) | copy-done | bytes 4120
  9.2 0.0 copy-start.6
  9.2 0.7 %copy-done.6 = s32[1,1,64]{2,1,0:T(1,128)S(1)} copy-done((s32[1,1,64]{2,1,0:T(1,128)S(1)}, s32[1,1,64]{2,1,0:T(1,128)}, u32[]{:S(2)}) %copy-start.6) | copy-done | bytes 280
  9.9 0.0 copy-start.7
  9.9 0.7 %copy-done.7 = f32[8]{0:T(128)S(1)} copy-done((f32[8]{0:T(128)S(1)}, f32[8]{0:T(128)}, u32[]{:S(2)}) %copy-start.7) | copy-done | bytes 56
  10.5 0.0 copy-start.8
  10.5 0.7 %copy-done.8 = s32[1,1,64]{2,1,0:T(1,128)S(1)} copy-done((s32[1,1,64]{2,1,0:T(1,128)S(1)}, s32[1,1,64]{2,1,0:T(1,128)}, u32[]{:S(2)}) %copy-start.8) | copy-done | bytes 280
  11.2 30.2 %shard_map.122 = (f32[1,3,32,16,512]{4,3,2,1,0:T(8,128)S(1)}, f32[1,16,512]{2,1,0:T(8,128)S(1)}) custom-call(f32[1,3,32,16,512]{4,3,2,1,0:T(8,128)S(1)} %copy-done.1, f32[1,16,512]{2,1,0:T(8,128)S(1)} %copy-done.2, s32[1,16,512]{2,1,0:T(8,128)S(1)} %copy-done.3, f32[1,32,32]{2,1,0:T(8,128)S(1)} %copy-done.5, f32[1,16,512]{2,1,0:T(8,128)S(1)} %copy-done.4, ...), custom_call_target="tpu_custom_call" | custom-call | tf_op jit(solution)/shard_map/pallas_call | solution.py:538
  41.4 1.7 %copy.17 = f32[1,3,32,16,512]{4,3,2,1,0:T(8,128)} copy(f32[1,3,32,16,512]{4,3,2,1,0:T(8,128)S(1)} %get-tuple-element.4) | data formatting | bytes 6291456
  43.1 0.6 %copy.18 = f32[1,16,512]{2,1,0:T(8,128)} copy(f32[1,16,512]{2,1,0:T(8,128)S(1)} %get-tuple-element.5) | data formatting | bytes 65536
Async XLA Ops:
  2.1 2.2 %copy-start = (bf16[1,1,64,256,128]{4,3,2,1,0:T(8,128)(2,1)S(1)}, bf16[1,1,64,256,128]{4,3,2,1,0:T(8,128)(2,1)}, u32[]{:S(2)}) copy-start(bf16[1,1,64,256,128]{4,3,2,1,0:T(8,128)(2,1)} %weights.1) | copy-start | bytes 12582916
  4.3 1.9 %copy-start.1 = (f32[1,3,32,16,512]{4,3,2,1,0:T(8,128)S(1)}, f32[1,3,32,16,512]{4,3,2,1,0:T(8,128)}, u32[]{:S(2)}) copy-start(f32[1,3,32,16,512]{4,3,2,1,0:T(8,128)} %state.1) | copy-start | bytes 9437188
  6.2 0.8 %copy-start.2 = (f32[1,16,512]{2,1,0:T(8,128)S(1)}, f32[1,16,512]{2,1,0:T(8,128)}, u32[]{:S(2)}) copy-start(f32[1,16,512]{2,1,0:T(8,128)} %speed.1) | copy-start | bytes 98308
  7.0 0.8 %copy-start.3 = (s32[1,16,512]{2,1,0:T(8,128)S(1)}, s32[1,16,512]{2,1,0:T(8,128)}, u32[]{:S(2)}) copy-start(s32[1,16,512]{2,1,0:T(8,128)} %mask.1) | copy-start | bytes 98308
  7.7 0.8 %copy-start.4 = (f32[1,16,512]{2,1,0:T(8,128)S(1)}, f32[1,16,512]{2,1,0:T(8,128)}, u32[]{:S(2)}) copy-start(f32[1,16,512]{2,1,0:T(8,128)} %temp.1) | copy-start | bytes 98308
  8.5 0.7 %copy-start.5 = (f32[1,32,32]{2,1,0:T(8,128)S(1)}, f32[1,32,32]{2,1,0:T(8,128)}, u32[]{:S(2)}) copy-start(f32[1,32,32]{2,1,0:T(8,128)} %vertical.1) | copy-start | bytes 12292
  9.2 0.7 %copy-start.6 = (s32[1,1,64]{2,1,0:T(1,128)S(1)}, s32[1,1,64]{2,1,0:T(1,128)}, u32[]{:S(2)}) copy-start(s32[1,1,64]{2,1,0:T(1,128)} %source_s.1) | copy-start | bytes 772
  9.9 0.7 %copy-start.7 = (f32[8]{0:T(128)S(1)}, f32[8]{0:T(128)}, u32[]{:S(2)}) copy-start(f32[8]{0:T(128)} %gain.1) | copy-start | bytes 100
  10.5 0.7 %copy-start.8 = (s32[1,1,64]{2,1,0:T(1,128)S(1)}, s32[1,1,64]{2,1,0:T(1,128)}, u32[]{:S(2)}) copy-start(s32[1,1,64]{2,1,0:T(1,128)} %target_in.1) | copy-start | bytes 772

commit v2 on v1

--- a/solution.py
+++ b/solution.py
@@ -39,6 +39,18 @@
     n_gx,
     n_gy,
     state,
+    speed_in,
+    mask_in,
+    vertical_in,
+    temp_in,
+    coef_in,
+    gain_in,
+    tile_hbm,
+    source_hbm,
+    target_hbm,
+    weights,
+    final,
+    surface,
     speed,
     mask,
     vertical,
@@ -48,10 +60,6 @@
     tile_in,
     source_in,
     target_in,
-    source_s,
-    weights,
-    final,
-    surface,
     raw,
     out,
     wbuf,
@@ -60,13 +68,18 @@
     u1,
     v1,
     p2,
+    rowsend,
+    rowrecv,
     colsend,
     colrecv,
     ybuf,
     yrecv,
     trecv,
     xbuf,
+    sbuf,
     load_sem,
+    small_sem,
+    surface_sem,
     w_sem,
     row_send,
     row_recv,
@@ -100,9 +113,29 @@
         part = pl.ds(i * per_chunk, per_chunk)
         return pltpu.make_async_copy(weights.at[0, 0, part], wbuf.at[part], w_sem.at[i])
 
-    for f in (1, 2, 0):
+    small = [
+        pltpu.make_async_copy(src, dst, small_sem.at[i])
+        for i, (src, dst) in enumerate(
+            (
+                (speed_in, speed),
+                (mask_in, mask),
+                (vertical_in, vertical),
+                (temp_in, temp),
+                (coef_in, coef),
+                (gain_in, gain),
+                (tile_hbm, tile_in),
+                (source_hbm, source_in),
+                (target_hbm, target_in),
+            )
+        )
+    ]
+    for f in (1, 2):
         for i in range(tiles):
             load(f, i).start()
+    for copy in small:
+        copy.start()
+    for i in range(tiles):
+        load(0, i).start()
     for i in range(CHUNKS):
         load_weights(i).start()
 
@@ -144,11 +177,10 @@
         for stage in range(4):
             colrecv[stage, 1] = jnp.zeros((levels, LANES), F32)
 
-    def row_copy(stage, buf, side):
-        src, dst = (1, rows + 1) if side == 0 else (rows, 0)
+    def row_copy(stage, side):
         return pltpu.make_async_remote_copy(
-            src_ref=buf.at[src],
-            dst_ref=buf.at[dst],
+            src_ref=rowsend.at[stage, side],
+            dst_ref=rowrecv.at[stage, 1 - side],
             send_sem=row_send.at[stage, side],
             recv_sem=row_recv.at[stage, side],
             device_id=(sec, a - 1 if side == 0 else a + 1, b),
@@ -173,7 +205,8 @@
 
             @pl.when(row_ok[side])
             def _(side=side):
-                row_copy(stage, buf, side).start()
+                rowsend[stage, side] = buf[rows if side else 1].astype(BF16)
+                row_copy(stage, side).start()
 
     def send_cols(stage):
         for side in range(2):
@@ -193,9 +226,10 @@
 
             @pl.when(row_ok[side])
             def _(side=side):
-                row_copy(stage, buf, 1 - side).wait_recv()
-
-    def wait_sent(stage, buf):
+                row_copy(stage, 1 - side).wait_recv()
+                buf[rows + 1 if side else 0] = rowrecv[stage, side].astype(F32)
+
+    def wait_sent(stage):
         for side in range(2):
 
             @pl.when(col_ok[side])
@@ -204,7 +238,7 @@
 
             @pl.when(row_ok[side])
             def _(side=side):
-                row_copy(stage, buf, side).wait_send()
+                row_copy(stage, side).wait_send()
 
     lane = iota((levels, LANES), 1)
 
@@ -243,10 +277,6 @@
         minus = jnp.concatenate([start, minus[:, LANES:]], axis=1)
         return plus - minus
 
-    m_high, m_low = split(vertical[0], 2)
-    m_high, m_low = m_high.astype(F32), m_low.astype(F32)
-    mixer = jnp.concatenate([m_high, m_high, m_low, m_low], axis=1).astype(BF16)
-
     def mix(right_side):
         high, low = split(right_side, 2)
         return right_side + dot(mixer, jnp.concatenate([high, low, high, low], axis=0))
@@ -258,10 +288,15 @@
     def sweep(row, after_edges, carry):
         carry = lax.fori_loop(0, 2, lambda i, c: row(i * (rows - 1), c), carry)
         after_edges()
-        carry = lax.fori_loop(
-            0, (rows - 2) // 2, lambda i, c: row(2 * i + 2, row(2 * i + 1, c)), carry
-        )
-        return carry
+        inner = rows - 2
+        step = next(k for k in (7, 6, 5, 4, 3, 2, 1) if inner % k == 0)
+
+        def several(i, c):
+            for k in range(step):
+                c = row(i * step + 1 + k, c)
+            return c
+
+        return lax.fori_loop(0, inner // step, several, carry)
 
     blank = jnp.zeros((levels, LANES), F32)
     pair = (blank, blank)
@@ -278,6 +313,11 @@
     send_rows(0, u0)
     loaded(2)
     start_cols(0, lax.fori_loop(0, rows, lambda x, c: pack(column(2, x), x, c), pair))
+    for copy in small:
+        copy.wait()
+    m_high, m_low = split(vertical[0], 2)
+    m_high, m_low = m_high.astype(F32), m_low.astype(F32)
+    mixer = jnp.concatenate([m_high, m_high, m_low, m_low], axis=1).astype(BF16)
     loaded(0)
 
     def wide_row(value):
@@ -295,8 +335,7 @@
         within = block_key(index & (out_blocks - 1), rows, out_per_row)
         return ((index >> shift) * out_blocks + within).astype(F32)
 
-    tile_col = tile_in[0, 0].astype(F32)
-    target_row = wide_row(target_in)
+    slot_row = wide_row(tile_in) * out_blocks + wide_row(target_in)
 
     def y_copy(t):
         return pltpu.make_async_remote_copy(
@@ -337,11 +376,12 @@
             jnp.concatenate([raw[f, i, 0] for i in range(tiles)], axis=1) for f in range(3)
         ] + [temp[0]]
         heat = jnp.zeros((rows, width), F32)
-        for f in range(coef.shape[0]):
-            total = coef[f, 0] * drivers[0]
+        factors, gains = coef[...], gain[...]
+        for f in range(factors.shape[1]):
+            total = factors[0:1, f : f + 1] * drivers[0]
             for k in range(1, 4):
-                total = total + coef[f, k] * drivers[k]
-            heat = heat + gain[f] * jnp.tanh(total).astype(BF16).astype(F32)
+                total = total + factors[k : k + 1, f : f + 1] * drivers[k]
+            heat = heat + gains[:, f : f + 1] * jnp.tanh(total).astype(BF16).astype(F32)
         blocks = jnp.concatenate(
             [heat[:, i * in_width : (i + 1) * in_width] for i in range(in_per_row)], axis=0
         )
@@ -364,11 +404,9 @@
                 group = jnp.where(sub == i + 1, both[:, out_width:], group)
             groups.append(group)
         heated = jnp.concatenate(groups, axis=0)
-        tile_row = jnp.sum(jnp.where(diagonal, tile_col, 0.0), axis=0, keepdims=True)
-        slot_row = tile_row * out_blocks + target_row
         placing = (slot_key(iota((slots, pairs), 0)) == slot_row).astype(F32).astype(BF16)
         dense = sum(dot(placing, piece) for piece in split(heated, 3))
-        ybuf[...] = dense.reshape(n_gx, out_blocks, out_width)
+        ybuf[...] = dense.astype(BF16).reshape(n_gx, out_blocks, out_width)
         for t in range(n_gx):
             y_copy(t).start()
 
@@ -416,7 +454,7 @@
                 device_id=(0, t, b),
                 device_id_type=MESH,
             ).wait_recv()
-            heating = heating + yrecv[t]
+            heating = heating + yrecv[t].astype(F32)
         ocean = as_blocks(temp[0]) + as_blocks(mask[0].astype(F32)) * heating
         trecv[a] = ocean.astype(BF16)
         for t in range(n_gx):
@@ -425,7 +463,7 @@
             def _():
                 t_copy(t).start()
 
-        surface[0] = jnp.concatenate(
+        sbuf[...] = jnp.concatenate(
             [ocean[i * rows : (i + 1) * rows] for i in range(out_per_row)], axis=1
         )
 
@@ -466,15 +504,16 @@
                     device_id_type=MESH,
                 ).wait_recv()
 
-        slot_col = tile_col * out_blocks + upright(target_row)
+        slot_col = upright(slot_row)
         picking = (slot_key(iota((pairs, slots), 1)) == slot_col).astype(F32).astype(BF16)
         returned = dot(picking, trecv[...].reshape(slots, out_width))
-        key = block_key(iota((in_blocks, out_width), 0), rows, in_per_row)
+        key = block_key(iota((in_blocks, pairs), 0), rows, in_per_row).astype(F32)
+        owner = (key == wide_row(source_in)).astype(F32)
         total = jnp.zeros((in_blocks, in_width), F32)
         for j in range(0, pairs, 2):
             left = jnp.concatenate(
                 [
-                    jnp.where(key == source_s[0, 0, i], returned[i : i + 1], 0.0)
+                    owner[:, i : i + 1] * returned[i : i + 1]
                     for i in (j, j + 1)
                 ],
                 axis=1,
@@ -499,15 +538,15 @@
     store_all(1)
     store_all(2)
 
-    for stage, buf in enumerate((u0, p1, u1, p2)):
-        wait_sent(stage, buf)
+    for stage in range(4):
+        wait_sent(stage)
 
     @pl.when(sec == 0)
     def _():
         for t in range(n_gx):
             y_copy(t).wait_send()
         x_copy().wait_recv()
-        surface[0] = xbuf[...]
+        sbuf[...] = xbuf[...]
 
     @pl.when(sec == 1)
     def _():
@@ -519,19 +558,24 @@
 
         x_copy().wait_send()
 
+    surface_copy = pltpu.make_async_copy(sbuf, surface.at[0], surface_sem)
+    surface_copy.start()
     for f in range(3):
         for i in range(tiles):
             store(f, i).wait()
+    surface_copy.wait()
 
 
 def local(n_gx, n_gy, *args):
     state, speed, mask, vertical, temp, coef, gain, tile, source, target, weights = args
+    coef = coef.T
+    gain = gain.reshape(1, -1)
+    tile = tile.reshape(source.shape)
     _, fields, levels, rows, width = state.shape
     pairs, in_width, out_width = weights.shape[2:]
     out_blocks = rows * width // out_width
-    vmem = pl.BlockSpec(memory_space=pltpu.VMEM)
-    smem = pl.BlockSpec(memory_space=pltpu.SMEM)
-    hbm = pl.BlockSpec(memory_space=pl.ANY)
+    hbm = pl.BlockSpec(memory_space=pltpu.HBM)
+    free = pl.BlockSpec(memory_space=pl.ANY)
     dma = pltpu.SemaphoreType.DMA
     tiled = pltpu.VMEM((fields, width // LANES, levels, rows, LANES), F32)
     tall = pltpu.VMEM((rows + 2, levels, width), F32)
@@ -541,9 +585,18 @@
             jax.ShapeDtypeStruct(state.shape, F32),
             jax.ShapeDtypeStruct(temp.shape, F32),
         ),
-        in_specs=[hbm, vmem, vmem, vmem, vmem, smem, smem, vmem, vmem, vmem, smem, hbm],
-        out_specs=(hbm, vmem),
+        in_specs=[hbm] * 11,
+        out_specs=(free, free),
         scratch_shapes=[
+            pltpu.VMEM(speed.shape, F32),
+            pltpu.VMEM(mask.shape, jnp.int32),
+            pltpu.VMEM(vertical.shape, F32),
+            pltpu.VMEM(temp.shape, F32),
+            pltpu.VMEM(coef.shape, F32),
+            pltpu.VMEM(gain.shape, F32),
+            pltpu.VMEM(tile.shape, jnp.int32),
+            pltpu.VMEM(source.shape, jnp.int32),
+            pltpu.VMEM(target.shape, jnp.int32),
             tiled,
             tiled,
             pltpu.VMEM((pairs, in_width, out_width), BF16),
@@ -552,13 +605,18 @@
             tall,
             pltpu.VMEM((rows, levels, width), F32),
             tall,
+            pltpu.VMEM((4, 2, levels, width), BF16),
+            pltpu.VMEM((4, 2, levels, width), BF16),
             pltpu.VMEM((4, 2, levels, LANES), F32),
             pltpu.VMEM((4, 2, levels, LANES), F32),
-            pltpu.VMEM((n_gx, out_blocks, out_width), F32),
-            pltpu.VMEM((n_gx, out_blocks, out_width), F32),
+            pltpu.VMEM((n_gx, out_blocks, out_width), BF16),
+            pltpu.VMEM((n_gx, out_blocks, out_width), BF16),
             pltpu.VMEM((n_gx, out_blocks, out_width), BF16),
             pltpu.VMEM((rows, width), F32),
+            pltpu.VMEM((rows, width), F32),
             dma((fields, width // LANES)),
+            dma((9,)),
+            dma(()),
             dma((CHUNKS,)),
             dma((4, 2)),
             dma((4, 2)),
@@ -573,9 +631,9 @@
             dma((fields, width // LANES)),
         ],
         compiler_params=pltpu.CompilerParams(
-            collective_id=0, has_side_effects=True, vmem_limit_bytes=40 * 2**20
+            collective_id=0, has_side_effects=True, vmem_limit_bytes=62 * 2**20
         ),
-    )(state, speed, mask, vertical, temp, coef, gain, tile, source, target, source, weights)
+    )(state, speed, mask, vertical, temp, coef, gain, tile, source, target, weights)
 
 
 def solution(mesh):

time: 44.2 us -> 33.1 us (0.75)
  local copies, waits for them, and re-layouts: 12.8 us -> 4.75 us
  Pallas kernels: 30.2 us -> 27.6 us
    unnamed x22 -> x4, local copies, waits for them, and re-layouts: 12.8 us -> 4.75 us
    pallas_call x1, Pallas kernels: 30.2 us -> 27.6 us  [local(): pl.pallas_call(functools.partial(kernel, n_gx, n_gy), out_shape=(jax.Shap...]
where the time goes in v2:
time: 33.1 us; the launch traced here: 33 us
  Pallas kernels  27.6 us (83%)
  local copies, waits for them, and re-layouts  4.75 us (14%)
  between operations  0.65 us (2%)
    pallas_call x1, Pallas kernels, local(): pl.pallas_call(functools.partial(kernel, n_gx, n_gy), out_shape=(jax.Shap...  27.6 us
    unnamed x4, local copies, waits for them, and re-layouts  4.75 us

profile of v2, /device:TPU:1, one launch (start us, length us, event | category | flops | bytes accessed | tf_op | source)
XLA Modules:
  0.0 33.0 jit_solution(2767407053423632586)
XLA Ops:
  0.6 27.6 %shard_map.122 = (f32[1,3,32,16,512]{4,3,2,1,0:T(8,128)}, f32[1,16,512]{2,1,0:T(8,128)}) custom-call(f32[1,3,32,16,512]{4,3,2,1,0:T(8,128)} %state.1, f32[1,16,512]{2,1,0:T(8,128)} %speed_in.1, s32[1,16,512]{2,1,0:T(8,128)} %mask_in.1, f32[1,32,32]{2,1,0:T(8,128)} %vertical_in.1, f32[1,16,512]{2,1,0:T(8,128)} %temp_in.1, f32[4,8]{1,0:T(4,128)} %bitcast.3, ...), custom_call_target="tpu_custom_call" | custom-call | tf_op jit(solution)/shard_map/pallas_call | solution.py:582
  28.2 0.0 copy-start
  28.2 4.1 %copy.15 = f32[1,3,32,16,512]{4,3,2,1,0:T(8,128)} copy(f32[1,3,32,16,512]{4,3,2,1,0:T(8,128)} %get-tuple-element.4) | data formatting | bytes 6291456
  32.4 0.0 copy-done
  32.4 0.6 %copy.16 = f32[1,16,512]{2,1,0:T(8,128)} copy(f32[1,16,512]{2,1,0:T(8,128)S(1)} %copy-done) | data formatting | bytes 65536
Async XLA Ops:
  28.2 4.1 %copy-start = (f32[1,16,512]{2,1,0:T(8,128)S(1)}, f32[1,16,512]{2,1,0:T(8,128)}, u32[]{:S(2)}) copy-start(f32[1,16,512]{2,1,0:T(8,128)} %get-tuple-element.5) | copy-start | bytes 98308

commit v3 on v2

--- a/solution.py
+++ b/solution.py
@@ -12,6 +12,10 @@
 BF16 = jnp.bfloat16
 LANES = 128
 CHUNKS = 8
+STAGES = 4
+MARGIN = 4
+P_FIELD, U_FIELD, V_FIELD = 0, 1, 2
+SPEED, MASK, P_COLS, V_COLS, U_COLS, U_BEFORE, U_AFTER = range(7)
 
 
 def iota(shape, axis):
@@ -49,7 +53,9 @@
     source_hbm,
     target_hbm,
     weights,
-    final,
+    p2_out,
+    u1_out,
+    v1_out,
     surface,
     speed,
     mask,
@@ -61,17 +67,24 @@
     source_in,
     target_in,
     raw,
-    out,
     wbuf,
     u0,
     p1,
     u1,
     v1,
     p2,
+    p_ext,
+    v_ext,
+    c_wide,
+    w_wide,
     rowsend,
     rowrecv,
     colsend,
-    colrecv,
+    u_recv,
+    v_recv,
+    p_recv,
+    speed_recv,
+    mask_recv,
     ybuf,
     yrecv,
     trecv,
@@ -147,98 +160,138 @@
             def _():
                 pl.semaphore_signal(barrier, inc=1, device_id=(s, t, b), device_id_type=MESH)
 
-    @pl.when(b > 0)
-    def _():
-        pl.semaphore_signal(barrier, inc=1, device_id=(sec, a, b - 1), device_id_type=MESH)
-
-    @pl.when(b < n_gy - 1)
-    def _():
-        pl.semaphore_signal(barrier, inc=1, device_id=(sec, a, b + 1), device_id_type=MESH)
+    row_ok = (a > 0, a < n_gx - 1)
+    col_ok = (b > 0, b < n_gy - 1)
+    both_ok = [[jnp.logical_and(r, c) for c in col_ok] for r in row_ok]
+
+    for side in range(2):
+        for dx in (-1, 0, 1):
+            near = col_ok[side] if dx == 0 else both_ok[(dx + 1) // 2][side]
+
+            @pl.when(near)
+            def _(side=side, dx=dx):
+                pl.semaphore_signal(
+                    barrier,
+                    inc=1,
+                    device_id=(sec, a + dx, b + 2 * side - 1),
+                    device_id_type=MESH,
+                )
 
     beside = (b > 0).astype(jnp.int32) + (b < n_gy - 1).astype(jnp.int32)
-
-    @pl.when(a == 0)
-    def _():
-        for buf in (u0, p1, u1, p2):
-            buf[0] = jnp.zeros((levels, width), F32)
-
-    @pl.when(a == n_gx - 1)
-    def _():
-        for buf in (u0, p1, u1, p2):
-            buf[rows + 1] = jnp.zeros((levels, width), F32)
-
-    @pl.when(b == 0)
-    def _():
-        for stage in range(4):
-            colrecv[stage, 0] = jnp.zeros((levels, LANES), F32)
-
-    @pl.when(b == n_gy - 1)
-    def _():
-        for stage in range(4):
-            colrecv[stage, 1] = jnp.zeros((levels, LANES), F32)
+    beside = beside * (1 + (a > 0).astype(jnp.int32) + (a < n_gx - 1).astype(jnp.int32))
+
+    for side in range(2):
+
+        @pl.when(jnp.logical_not(row_ok[side]))
+        def _(side=side):
+            for buf in (u0, p1, u1, p2):
+                buf[side * (rows + 1)] = jnp.zeros(buf.shape[1:], F32)
+            for other in range(2):
+                u_recv[2 * side, other] = jnp.zeros((levels, LANES), F32)
+
+        @pl.when(jnp.logical_not(col_ok[side]))
+        def _(side=side):
+            for dx in range(3):
+                u_recv[dx, side] = jnp.zeros((levels, LANES), F32)
+            v_recv[side] = jnp.zeros((levels, LANES), F32)
+            p_recv[side] = jnp.zeros((levels, LANES), F32)
+            speed_recv[side] = jnp.zeros((rows, LANES), F32)
+            mask_recv[side] = jnp.zeros((rows, LANES), jnp.int32)
 
     def row_copy(stage, side):
+        src, dst = rowsend.at[stage, side], rowrecv.at[stage, 1 - side]
+        if stage == 0:
+            src, dst = src.at[:, pl.ds(0, width)], dst.at[:, pl.ds(0, width)]
         return pltpu.make_async_remote_copy(
-            src_ref=rowsend.at[stage, side],
-            dst_ref=rowrecv.at[stage, 1 - side],
+            src_ref=src,
+            dst_ref=dst,
             send_sem=row_send.at[stage, side],
             recv_sem=row_recv.at[stage, side],
             device_id=(sec, a - 1 if side == 0 else a + 1, b),
             device_id_type=MESH,
         )
 
-    def col_copy(stage, side):
+    def col_copy(kind, side):
+        edge = pl.ds(0 if side == 0 else width - LANES, LANES)
+        other = 1 - side
+        src, dst = {
+            SPEED: (speed.at[0, :, edge], speed_recv.at[other]),
+            MASK: (mask.at[0, :, edge], mask_recv.at[other]),
+            P_COLS: (colsend.at[P_FIELD, side], p_recv.at[other]),
+            V_COLS: (colsend.at[V_FIELD, side], v_recv.at[other]),
+            U_COLS: (colsend.at[U_FIELD, side], u_recv.at[1, other]),
+            U_BEFORE: (colsend.at[U_FIELD, side], u_recv.at[2, other]),
+            U_AFTER: (colsend.at[U_FIELD, side], u_recv.at[0, other]),
+        }[kind]
+        to = {U_BEFORE: a - 1, U_AFTER: a + 1}.get(kind, a)
         return pltpu.make_async_remote_copy(
-            src_ref=colsend.at[stage, side],
-            dst_ref=colrecv.at[stage, 1 - side],
-            send_sem=col_send.at[stage, side],
-            recv_sem=col_recv.at[stage, side],
-            device_id=(sec, a, b - 1 if side == 0 else b + 1),
+            src_ref=src,
+            dst_ref=dst,
+            send_sem=col_send.at[kind, side],
+            recv_sem=col_recv.at[kind, side],
+            device_id=(sec, to, b - 1 if side == 0 else b + 1),
             device_id_type=MESH,
         )
 
-    row_ok = (a > 0, a < n_gx - 1)
-    col_ok = (b > 0, b < n_gy - 1)
+    def col_sends(kind, side):
+        return {U_BEFORE: both_ok[0], U_AFTER: both_ok[1]}.get(kind, col_ok)[side]
+
+    def col_comes(kind, side):
+        return {U_BEFORE: both_ok[1], U_AFTER: both_ok[0]}.get(kind, col_ok)[side]
 
     def send_rows(stage, buf):
+        span = width if stage == 0 else width + LANES
         for side in range(2):
 
             @pl.when(row_ok[side])
             def _(side=side):
-                rowsend[stage, side] = buf[rows if side else 1].astype(BF16)
+                edge = buf[rows if side else 1]
+                rowsend[stage, side, :, :span] = edge[:, :span].astype(BF16)
                 row_copy(stage, side).start()
 
-    def send_cols(stage):
-        for side in range(2):
-
-            @pl.when(col_ok[side])
-            def _(side=side):
-                col_copy(stage, side).start()
-
-    def wait_halo(stage, buf):
-        for side in range(2):
-
-            @pl.when(col_ok[side])
-            def _(side=side):
-                col_copy(stage, 1 - side).wait_recv()
-
+    def send_cols(*kinds):
+        for kind in kinds:
+            for side in range(2):
+
+                @pl.when(col_sends(kind, side))
+                def _(side=side, kind=kind):
+                    col_copy(kind, side).start()
+
+    def wait_cols():
+        for kind in range(7):
+            for side in range(2):
+
+                @pl.when(col_comes(kind, side))
+                def _(side=side, kind=kind):
+                    col_copy(kind, 1 - side).wait_recv()
+
+    def wait_rows(stage, buf):
         for side in range(2):
 
             @pl.when(row_ok[side])
             def _(side=side):
                 row_copy(stage, 1 - side).wait_recv()
-                buf[rows + 1 if side else 0] = rowrecv[stage, side].astype(F32)
-
-    def wait_sent(stage):
+                at = rows + 1 if side else 0
+                if stage == 0:
+                    buf[at, :, :width] = rowrecv[stage, side, :, :width].astype(F32)
+                    near = u_recv.at[2 * side]
+                    buf[at, :, width:] = margin(near, 0 if side else rows - 1)
+                else:
+                    buf[at] = rowrecv[stage, side].astype(F32)
+
+    def wait_sent():
         for side in range(2):
-
-            @pl.when(col_ok[side])
-            def _(side=side):
-                col_copy(stage, side).wait_send()
-
-            @pl.when(row_ok[side])
-            def _(side=side):
-                row_copy(stage, side).wait_send()
+            for kind in range(7):
+
+                @pl.when(col_sends(kind, side))
+                def _(side=side, kind=kind):
+                    col_copy(kind, side).wait_send()
+
+            for stage in range(STAGES):
+
+                @pl.when(row_ok[side])
+                def _(side=side, stage=stage):
+                    row_copy(stage, side).wait_send()
 
     lane = iota((levels, LANES), 1)
 
@@ -246,79 +299,92 @@
         return [buf.at[f, i].reshape(levels * rows, LANES) for i in range(tiles)]
 
     flat_raw = [flat(raw, f) for f in range(3)]
-    flat_out = [flat(out, f) for f in range(3)]
 
     def column(f, x):
         parts = [ref[pl.ds(x, levels, stride=rows), :] for ref in flat_raw[f]]
         return jnp.concatenate(parts, axis=1)
 
-    def put(f, x, value):
-        for i, ref in enumerate(flat_out[f]):
-            ref[pl.ds(x, levels, stride=rows), :] = value[:, i * LANES : (i + 1) * LANES]
+    def edges(f, x):
+        return [flat_raw[f][i][pl.ds(x, levels, stride=rows), :] for i in (0, tiles - 1)]
 
     def loaded(f):
         for i in range(tiles):
             load(f, i).wait()
 
-    def pack(value, x, carry):
+    mine = lane // MARGIN
+
+    def pack(f, x, carry):
         low, high = carry
-        low = jnp.where(lane == x, pltpu.roll(value[:, :LANES], x, 1), low)
-        high = jnp.where(lane == x, pltpu.roll(value[:, width - LANES :], x + 1, 1), high)
+        first, last = edges(f, x)
+        low = jnp.where(mine == x, pltpu.roll(first, MARGIN * x, 1), low)
+        high = jnp.where(mine == x, pltpu.roll(last, MARGIN * x + MARGIN, 1), high)
         return low, high
 
-    def along_y(value, stage, x):
-        left = pltpu.roll(colrecv[stage, 0], lax.rem(LANES - x, LANES), 1)
-        right = pltpu.roll(colrecv[stage, 1], LANES - 1 - x, 1)
-        plus = pltpu.roll(value, width - 1, 1)
-        minus = pltpu.roll(value, 1, 1)
-        end = jnp.where(lane == LANES - 1, right, plus[:, width - LANES :])
-        start = jnp.where(lane == 0, left, minus[:, :LANES])
-        plus = jnp.concatenate([plus[:, : width - LANES], end], axis=1)
-        minus = jnp.concatenate([start, minus[:, LANES:]], axis=1)
-        return plus - minus
+    def pack_all(f):
+        blank = jnp.zeros((levels, LANES), F32)
+
+        def several(i, carry):
+            for k in range(4):
+                carry = pack(f, 4 * i + k, carry)
+            return carry
+
+        low, high = lax.fori_loop(0, rows // 4, several, (blank, blank))
+        colsend[f, 0] = low
+        colsend[f, 1] = high
+
+    def margin(ref, x):
+        before = pltpu.roll(ref[0], LANES - MARGIN - MARGIN * x, 1)
+        after = pltpu.roll(ref[1], lax.rem(LANES - MARGIN * x, LANES), 1)
+        rest = jnp.where(lane >= LANES - MARGIN, before, 0.0)
+        return jnp.where(lane < MARGIN, after, rest)
+
+    def along_y(value):
+        return pltpu.roll(value, value.shape[1] - 1, 1) - pltpu.roll(value, 1, 1)
 
     def mix(right_side):
         high, low = split(right_side, 2)
         return right_side + dot(mixer, jnp.concatenate([high, low, high, low], axis=0))
 
-    def pressure_row(stage, x, p, u_buf, v):
-        divergence = (u_buf[x + 2] - u_buf[x]) + along_y(v, stage, x)
-        return mix(p - speed[0, pl.ds(x, 1), :] * divergence)
-
-    def sweep(row, after_edges, carry):
-        carry = lax.fori_loop(0, 2, lambda i, c: row(i * (rows - 1), c), carry)
+    def pressure_row(x, p, u_buf, v):
+        divergence = (u_buf[x + 2] - u_buf[x]) + along_y(v)
+        return mix(p - c_wide[pl.ds(x, 1), :] * divergence)
+
+    def sweep(row, after_edges):
+        def edge(i, c):
+            row(i * (rows - 1))
+            return c
+
+        lax.fori_loop(0, 2, edge, 0)
         after_edges()
         inner = rows - 2
         step = next(k for k in (7, 6, 5, 4, 3, 2, 1) if inner % k == 0)
 
         def several(i, c):
             for k in range(step):
-                c = row(i * step + 1 + k, c)
+                row(i * step + 1 + k)
             return c
 
-        return lax.fori_loop(0, inner // step, several, carry)
-
-    blank = jnp.zeros((levels, LANES), F32)
-    pair = (blank, blank)
-
-    def start_cols(stage, carry):
-        colsend[stage, 0] = carry[0]
-        colsend[stage, 1] = carry[1]
-        send_cols(stage)
-
-    loaded(1)
-    u0[1] = column(1, 0)
-    u0[rows] = column(1, rows - 1)
+        lax.fori_loop(0, inner // step, several, 0)
+
+    loaded(U_FIELD)
+    u0[1, :, :width] = column(U_FIELD, 0)
+    u0[rows, :, :width] = column(U_FIELD, rows - 1)
     pl.semaphore_wait(barrier, 2 * n_gx - 1 + beside)
     send_rows(0, u0)
-    loaded(2)
-    start_cols(0, lax.fori_loop(0, rows, lambda x, c: pack(column(2, x), x, c), pair))
+    pack_all(U_FIELD)
+    send_cols(U_COLS, U_BEFORE, U_AFTER)
+    loaded(V_FIELD)
+    pack_all(V_FIELD)
+    send_cols(V_COLS)
     for copy in small:
         copy.wait()
+    send_cols(SPEED, MASK)
+    loaded(P_FIELD)
+    pack_all(P_FIELD)
+    send_cols(P_COLS)
     m_high, m_low = split(vertical[0], 2)
     m_high, m_low = m_high.astype(F32), m_low.astype(F32)
     mixer = jnp.concatenate([m_high, m_high, m_low, m_low], axis=1).astype(BF16)
-    loaded(0)
 
     def wide_row(value):
         return value[0, 0].reshape(1, pairs).astype(F32)
@@ -411,31 +477,59 @@
             y_copy(t).start()
 
     def fill(x, c):
-        u0[x + 1] = column(1, x)
+        u0[x + 1, :, :width] = column(U_FIELD, x)
         return c
 
     lax.fori_loop(1, rows - 1, fill, 0)
-    wait_halo(0, u0)
-
-    def first_pressure(x, c):
-        p = pressure_row(0, x, column(0, x), u0, column(2, x))
-        p1[x + 1] = p
-        return pack(p, x, c)
-
-    start_cols(1, sweep(first_pressure, lambda: send_rows(1, p1), pair))
-    wait_halo(1, p1)
-
-    def free(x):
-        return mask[0, pl.ds(x, 1), :].astype(F32)
-
-    def first_velocity(x, c):
-        w = free(x)
+    wait_cols()
+
+    def fill_margins(x, c):
+        u0[x + 1, :, width:] = margin(u_recv.at[1], x)
+        v_ext[x] = margin(v_recv, x)
+        p_ext[x] = margin(p_recv, x)
+        return c
+
+    lax.fori_loop(0, rows, fill_margins, 0)
+    across = iota((rows, LANES), 1)
+
+    def around(pair):
+        rest = jnp.where(across >= LANES - MARGIN, pair[0], 0.0)
+        return jnp.where(across < MARGIN, pair[1], rest)
+
+    c_wide[:, :width] = speed[0]
+    c_wide[:, width:] = around(speed_recv[...])
+    w_wide[:, :width] = mask[0].astype(F32)
+    w_wide[:, width:] = around(mask_recv[...].astype(F32))
+    wait_rows(0, u0)
+
+    def wide_column(f, ext, x):
+        return jnp.concatenate([column(f, x), ext[x]], axis=1)
+
+    def first_pressure(x):
+        p = wide_column(P_FIELD, p_ext, x)
+        p1[x + 1] = pressure_row(x, p, u0, wide_column(V_FIELD, v_ext, x))
+
+    sweep(first_pressure, lambda: send_rows(1, p1))
+    wait_rows(1, p1)
+
+    def first_velocity(x):
+        w = w_wide[pl.ds(x, 1), :]
         u1[x + 1] = w * (u0[x + 1] - 0.5 * (p1[x + 2] - p1[x]))
-        v = w * (column(2, x) - 0.5 * along_y(p1[x + 1], 1, x))
-        v1[x] = v
-        return pack(v, x, c)
-
-    start_cols(2, sweep(first_velocity, lambda: send_rows(2, u1), pair))
+        v1[x] = w * (wide_column(V_FIELD, v_ext, x) - 0.5 * along_y(p1[x + 1]))
+
+    sweep(first_velocity, lambda: send_rows(2, u1))
+
+    near = pl.ds(0, width)
+    inner = pl.ds(1, rows)
+    stores = [
+        pltpu.make_async_copy(u1.at[inner, :, near], u1_out, out_sem.at[0]),
+        pltpu.make_async_copy(v1.at[:, :, near], v1_out, out_sem.at[1]),
+        pltpu.make_async_copy(p2.at[inner], p2_out.at[inner], out_sem.at[2]),
+        pltpu.make_async_copy(p2.at[0], p2_out.at[0], out_sem.at[3]),
+        pltpu.make_async_copy(p2.at[rows + 1], p2_out.at[rows + 1], out_sem.at[4]),
+    ]
+    stores[0].start()
+    stores[1].start()
 
     def as_blocks(value):
         return jnp.concatenate(
@@ -467,25 +561,13 @@
             [ocean[i * rows : (i + 1) * rows] for i in range(out_per_row)], axis=1
         )
 
-    wait_halo(2, u1)
-
-    def second_pressure(x, c):
-        p = pressure_row(2, x, p1[x + 1], u1, v1[x])
-        p2[x + 1] = p
-        put(0, x, p)
-        return pack(p, x, c)
-
-    start_cols(3, sweep(second_pressure, lambda: send_rows(3, p2), pair))
-
-    def store(f, i):
-        part = final.at[0, f, :, :, pl.ds(i * LANES, LANES)]
-        return pltpu.make_async_copy(out.at[f, i], part, out_sem.at[f, i])
-
-    def store_all(f):
-        for i in range(tiles):
-            store(f, i).start()
-
-    store_all(0)
+    wait_rows(2, u1)
+
+    def second_pressure(x):
+        p2[x + 1] = pressure_row(x, p1[x + 1], u1, v1[x])
+
+    sweep(second_pressure, lambda: send_rows(3, p2))
+    stores[2].start()
 
     @pl.when(sec == 1)
     def _():
@@ -526,20 +608,10 @@
         )
         x_copy().start()
 
-    wait_halo(3, p2)
-
-    def second_velocity(x, c):
-        w = free(x)
-        put(1, x, w * (u1[x + 1] - 0.5 * (p2[x + 2] - p2[x])))
-        put(2, x, w * (v1[x] - 0.5 * along_y(p2[x + 1], 3, x)))
-        return c
-
-    sweep(second_velocity, lambda: None, 0)
-    store_all(1)
-    store_all(2)
-
-    for stage in range(4):
-        wait_sent(stage)
+    wait_rows(3, p2)
+    stores[3].start()
+    stores[4].start()
+    wait_sent()
 
     @pl.when(sec == 0)
     def _():
@@ -560,9 +632,91 @@
 
     surface_copy = pltpu.make_async_copy(sbuf, surface.at[0], surface_sem)
     surface_copy.start()
-    for f in range(3):
-        for i in range(tiles):
-            store(f, i).wait()
+    for copy in stores:
+        copy.wait()
+    surface_copy.wait()
+
+
+def last_kernel(
+    p_in,
+    u_in,
+    v_in,
+    mask_in,
+    surface_in,
+    final,
+    surface,
+    p,
+    u,
+    v,
+    mask,
+    out,
+    sem,
+    out_sem,
+    small_sem,
+):
+    rows, levels, width = u_in.shape
+    tiles = width // LANES
+    parts = rows // 4
+    half = 8
+
+    mask_copy = pltpu.make_async_copy(mask_in, mask, small_sem.at[0])
+    surface_copy = pltpu.make_async_copy(surface_in, surface, small_sem.at[1])
+    mask_copy.start()
+    loads = []
+    for k in range(parts):
+        first = 0 if k == 0 else 4 * k + 2
+        p_rows = pl.ds(first, 4 * k + 6 - first)
+        part = pl.ds(4 * k, 4)
+        loads.append(
+            [
+                pltpu.make_async_copy(src, dst, sem.at[k, i])
+                for i, (src, dst) in enumerate(
+                    (
+                        (p_in.at[p_rows], p.at[p_rows]),
+                        (u_in.at[part], u.at[part]),
+                        (v_in.at[part], v.at[part]),
+                    )
+                )
+            ]
+        )
+        for copy in loads[-1]:
+            copy.start()
+    surface_copy.start()
+    mask_copy.wait()
+
+    def store(h, f, i):
+        part = final.at[0, f, :, pl.ds(h * half, half), pl.ds(i * LANES, LANES)]
+        return pltpu.make_async_copy(out.at[h, f, i], part, out_sem.at[h, f, i])
+
+    stores = [store(h, f, i) for h in range(rows // half) for f in range(3) for i in range(tiles)]
+    for k in range(parts):
+        for copy in loads[k]:
+            copy.wait()
+        for x in range(4 * k, 4 * k + 4):
+            h = x // half
+            w = mask[0, x : x + 1, :].astype(F32)
+            here = p[x + 1]
+            span = here.shape[1]
+            plus = pltpu.roll(here, span - 1, 1)[:, :width]
+            minus = pltpu.roll(here, 1, 1)[:, :width]
+            gradient = p[x + 2, :, :width] - p[x, :, :width]
+            values = (
+                here[:, :width],
+                w * (u[x] - 0.5 * gradient),
+                w * (v[x] - 0.5 * (plus - minus)),
+            )
+            for f, value in enumerate(values):
+                for i in range(tiles):
+                    flat = out.at[h, f, i].reshape(levels * half, LANES)
+                    at = pl.ds(x % half, levels, stride=half)
+                    flat[at, :] = value[:, i * LANES : (i + 1) * LANES]
+        if (4 * k + 4) % half == 0:
+            per_half = 3 * tiles
+            h = (4 * k + 4) // half - 1
+            for copy in stores[h * per_half : (h + 1) * per_half]:
+                copy.start()
+    for copy in stores:
+        copy.wait()
     surface_copy.wait()
 
 
@@ -578,15 +732,20 @@
     free = pl.BlockSpec(memory_space=pl.ANY)
     dma = pltpu.SemaphoreType.DMA
     tiled = pltpu.VMEM((fields, width // LANES, levels, rows, LANES), F32)
-    tall = pltpu.VMEM((rows + 2, levels, width), F32)
-    return pl.pallas_call(
+    span = width + LANES
+    tall = pltpu.VMEM((rows + 2, levels, span), F32)
+    ext = pltpu.VMEM((rows, levels, LANES), F32)
+    params = dict(has_side_effects=True, vmem_limit_bytes=62 * 2**20)
+    p2, u1, v1, surface = pl.pallas_call(
         functools.partial(kernel, n_gx, n_gy),
         out_shape=(
-            jax.ShapeDtypeStruct(state.shape, F32),
+            jax.ShapeDtypeStruct((rows + 2, levels, span), F32),
+            jax.ShapeDtypeStruct((rows, levels, width), F32),
+            jax.ShapeDtypeStruct((rows, levels, width), F32),
             jax.ShapeDtypeStruct(temp.shape, F32),
         ),
         in_specs=[hbm] * 11,
-        out_specs=(free, free),
+        out_specs=(free,) * 4,
         scratch_shapes=[
             pltpu.VMEM(speed.shape, F32),
             pltpu.VMEM(mask.shape, jnp.int32),
@@ -598,17 +757,24 @@
             pltpu.VMEM(source.shape, jnp.int32),
             pltpu.VMEM(target.shape, jnp.int32),
             tiled,
-            tiled,
             pltpu.VMEM((pairs, in_width, out_width), BF16),
             tall,
             tall,
             tall,
-            pltpu.VMEM((rows, levels, width), F32),
+            pltpu.VMEM((rows, levels, span), F32),
             tall,
-            pltpu.VMEM((4, 2, levels, width), BF16),
-            pltpu.VMEM((4, 2, levels, width), BF16),
-            pltpu.VMEM((4, 2, levels, LANES), F32),
-            pltpu.VMEM((4, 2, levels, LANES), F32),
+            ext,
+            ext,
+            pltpu.VMEM((rows, span), F32),
+            pltpu.VMEM((rows, span), F32),
+            pltpu.VMEM((STAGES, 2, levels, span), BF16),
+            pltpu.VMEM((STAGES, 2, levels, span), BF16),
+            pltpu.VMEM((fields, 2, levels, LANES), F32),
+            pltpu.VMEM((3, 2, levels, LANES), F32),
+            pltpu.VMEM((2, levels, LANES), F32),
+            pltpu.VMEM((2, levels, LANES), F32),
+            pltpu.VMEM((2, rows, LANES), F32),
+            pltpu.VMEM((2, rows, LANES), jnp.int32),
             pltpu.VMEM((n_gx, out_blocks, out_width), BF16),
             pltpu.VMEM((n_gx, out_blocks, out_width), BF16),
             pltpu.VMEM((n_gx, out_blocks, out_width), BF16),
@@ -618,22 +784,40 @@
             dma((9,)),
             dma(()),
             dma((CHUNKS,)),
-            dma((4, 2)),
-            dma((4, 2)),
-            dma((4, 2)),
-            dma((4, 2)),
+            dma((STAGES, 2)),
+            dma((STAGES, 2)),
+            dma((7, 2)),
+            dma((7, 2)),
             dma((n_gx,)),
             dma((n_gx,)),
             dma((n_gx,)),
             dma((n_gx,)),
             dma(()),
             dma(()),
-            dma((fields, width // LANES)),
+            dma((5,)),
         ],
-        compiler_params=pltpu.CompilerParams(
-            collective_id=0, has_side_effects=True, vmem_limit_bytes=62 * 2**20
+        compiler_params=pltpu.CompilerParams(collective_id=0, **params),
+    )(state, speed, mask, vertical, temp, coef, gain, tile, source, target, weights)
+    return pl.pallas_call(
+        last_kernel,
+        out_shape=(
+            jax.ShapeDtypeStruct(state.shape, F32),
+            jax.ShapeDtypeStruct(temp.shape, F32),
         ),
-    )(state, speed, mask, vertical, temp, coef, gain, tile, source, target, weights)
+        in_specs=[hbm] * 5,
+        out_specs=(free, free),
+        scratch_shapes=[
+            tall,
+            pltpu.VMEM((rows, levels, width), F32),
+            pltpu.VMEM((rows, levels, width), F32),
+            pltpu.VMEM(mask.shape, jnp.int32),
+            pltpu.VMEM((rows // 8, fields, width // LANES, levels, 8, LANES), F32),
+            dma((rows // 4, 3)),
+            dma((rows // 8, fields, width // LANES)),
+            dma((2,)),
+        ],
+        compiler_params=pltpu.CompilerParams(**params),
+    )(p2, u1, v1, mask, surface)
 
 
 def solution(mesh):

time: 33.1 us -> 29.4 us (0.89)
  the two profiles are of different devices: /device:TPU:1 before, /device:TPU:0 now
where the time goes in v3:
time: 29.4 us; the launch traced here: 29.3 us
  Pallas kernels  28.7 us (98%)
  between operations  0.64 us (2%)
    pallas_call x1, Pallas kernels, local(): pl.pallas_call(functools.partial(kernel, n_gx, n_gy), out_shape=(jax.Shap...  24.3 us
    pallas_call x1, Pallas kernels, local(): pl.pallas_call(last_kernel, out_shape=(jax.ShapeDtypeStruct(state.shape,...  4.4 us

profile of v3, /device:TPU:0, one launch (start us, length us, event | category | flops | bytes accessed | tf_op | source)
XLA Modules:
  0.0 29.3 jit_solution(245227864915398632)
XLA Ops:
  0.6 24.3 %shard_map.122 = (f32[18,32,640]{2,1,0:T(8,128)}, f32[16,32,512]{2,1,0:T(8,128)}, f32[16,32,512]{2,1,0:T(8,128)}, f32[1,16,512]{2,1,0:T(8,128)}) custom-call(f32[1,3,32,16,512]{4,3,2,1,0:T(8,128)} %state.1, f32[1,16,512]{2,1,0:T(8,128)} %speed_in.1, s32[1,16,512]{2,1,0:T(8,128)} %mask_in.3, f32[1,32,32]{2,1,0:T(8,128)} %vertical_in.1, ...), custom_call_target="tpu_custom_call" | custom-call | tf_op jit(solution)/shard_map/pallas_call | solution.py:739
  24.9 4.4 %shard_map.123 = (f32[1,3,32,16,512]{4,3,2,1,0:T(8,128)}, f32[1,16,512]{2,1,0:T(8,128)}) custom-call(f32[18,32,640]{2,1,0:T(8,128)} %get-tuple-element.6.p_in, f32[16,32,512]{2,1,0:T(8,128)} %get-tuple-element.7.u_in, f32[16,32,512]{2,1,0:T(8,128)} %get-tuple-element.8.v_in, s32[1,16,512]{2,1,0:T(8,128)} %mask_in.3, f32[1,16,512]{2,1,0:T(8,128)} %get-tuple-element.9.surface_in), custom_call_target="tpu_custom_call" | custom-call | tf_op jit(solution)/shard_map/pallas_call | solution.py:801

commit v4 on v3

--- a/solution.py
+++ b/solution.py
@@ -37,6 +37,25 @@
 
 def block_key(index, rows, per_row):
     return (index & (rows - 1)) * per_row + (index >> (rows.bit_length() - 1))
+
+
+def wide_row(ref):
+    return ref[0, 0].reshape(1, ref.shape[-1]).astype(F32)
+
+
+def upright(row):
+    size = row.shape[1]
+    diagonal = iota((size, size), 0) == iota((size, size), 1)
+    return jnp.sum(jnp.where(diagonal, row, 0.0), axis=1, keepdims=True)
+
+
+def slot_key(index, blocks, rows, per_row):
+    within = block_key(index & (blocks - 1), rows, per_row)
+    return ((index >> (blocks.bit_length() - 1)) * blocks + within).astype(F32)
+
+
+def wide(weights, j):
+    return jnp.concatenate([weights[j], weights[j + 1]], axis=1)
 
 
 def kernel(
@@ -57,6 +76,7 @@
     u1_out,
     v1_out,
     surface,
+    returned,
     speed,
     mask,
     vertical,
@@ -87,8 +107,8 @@
     mask_recv,
     ybuf,
     yrecv,
+    tsend,
     trecv,
-    xbuf,
     sbuf,
     load_sem,
     small_sem,
@@ -102,8 +122,6 @@
     y_recv,
     t_send,
     t_recv,
-    x_send,
-    x_recv,
     out_sem,
 ):
     sec = lax.axis_index("sec")
@@ -149,8 +167,11 @@
         copy.start()
     for i in range(tiles):
         load(0, i).start()
-    for i in range(CHUNKS):
-        load_weights(i).start()
+
+    @pl.when(sec == 0)
+    def _():
+        for i in range(CHUNKS):
+            load_weights(i).start()
 
     barrier = pltpu.get_barrier_semaphore()
     for s in range(2):
@@ -386,21 +407,7 @@
     m_high, m_low = m_high.astype(F32), m_low.astype(F32)
     mixer = jnp.concatenate([m_high, m_high, m_low, m_low], axis=1).astype(BF16)
 
-    def wide_row(value):
-        return value[0, 0].reshape(1, pairs).astype(F32)
-
-    diagonal = iota((pairs, pairs), 0) == iota((pairs, pairs), 1)
-
-    def upright(row):
-        return jnp.sum(jnp.where(diagonal, row, 0.0), axis=1, keepdims=True)
-
     slots = n_gx * out_blocks
-    shift = out_blocks.bit_length() - 1
-
-    def slot_key(index):
-        within = block_key(index & (out_blocks - 1), rows, out_per_row)
-        return ((index >> shift) * out_blocks + within).astype(F32)
-
     slot_row = wide_row(tile_in) * out_blocks + wide_row(target_in)
 
     def y_copy(t):
@@ -413,28 +420,15 @@
             device_id_type=MESH,
         )
 
-    def x_copy():
-        return pltpu.make_async_remote_copy(
-            src_ref=xbuf,
-            dst_ref=xbuf,
-            send_sem=x_send,
-            recv_sem=x_recv,
-            device_id=(0, a, b),
-            device_id_type=MESH,
-        )
-
     def t_copy(t):
         return pltpu.make_async_remote_copy(
-            src_ref=trecv.at[a],
+            src_ref=tsend,
             dst_ref=trecv.at[a],
             send_sem=t_send.at[t],
             recv_sem=t_recv.at[a],
-            device_id=(1, t, b),
+            device_id=(0, t, b),
             device_id_type=MESH,
         )
-
-    def wide(j):
-        return jnp.concatenate([wbuf[j], wbuf[j + 1]], axis=1)
 
     @pl.when(sec == 0)
     def _():
@@ -464,13 +458,13 @@
             left = jnp.concatenate([high[part], low[part]], axis=0).astype(BF16)
             group = jnp.zeros((8, out_width), F32)
             for i in range(0, 8, 2):
-                both = dot(left, wide(8 * g + i))
+                both = dot(left, wide(wbuf, 8 * g + i))
                 both = both[:8] + both[8:]
                 group = jnp.where(sub == i, both[:, :out_width], group)
                 group = jnp.where(sub == i + 1, both[:, out_width:], group)
             groups.append(group)
         heated = jnp.concatenate(groups, axis=0)
-        placing = (slot_key(iota((slots, pairs), 0)) == slot_row).astype(F32).astype(BF16)
+        placing = (slot_key(iota((slots, pairs), 0), out_blocks, rows, out_per_row) == slot_row).astype(F32).astype(BF16)
         dense = sum(dot(placing, piece) for piece in split(heated, 3))
         ybuf[...] = dense.astype(BF16).reshape(n_gx, out_blocks, out_width)
         for t in range(n_gx):
@@ -550,12 +544,9 @@
             ).wait_recv()
             heating = heating + yrecv[t].astype(F32)
         ocean = as_blocks(temp[0]) + as_blocks(mask[0].astype(F32)) * heating
-        trecv[a] = ocean.astype(BF16)
+        tsend[...] = ocean.astype(BF16)
         for t in range(n_gx):
-
-            @pl.when(t != a)
-            def _():
-                t_copy(t).start()
+            t_copy(t).start()
 
         sbuf[...] = jnp.concatenate(
             [ocean[i * rows : (i + 1) * rows] for i in range(out_per_row)], axis=1
@@ -568,45 +559,6 @@
 
     sweep(second_pressure, lambda: send_rows(3, p2))
     stores[2].start()
-
-    @pl.when(sec == 1)
-    def _():
-        for i in range(CHUNKS):
-            load_weights(i).wait()
-        for t in range(n_gx):
-
-            @pl.when(t != a)
-            def _():
-                pltpu.make_async_remote_copy(
-                    src_ref=trecv.at[t],
-                    dst_ref=trecv.at[t],
-                    send_sem=t_send.at[t],
-                    recv_sem=t_recv.at[t],
-                    device_id=(1, t, b),
-                    device_id_type=MESH,
-                ).wait_recv()
-
-        slot_col = upright(slot_row)
-        picking = (slot_key(iota((pairs, slots), 1)) == slot_col).astype(F32).astype(BF16)
-        returned = dot(picking, trecv[...].reshape(slots, out_width))
-        key = block_key(iota((in_blocks, pairs), 0), rows, in_per_row).astype(F32)
-        owner = (key == wide_row(source_in)).astype(F32)
-        total = jnp.zeros((in_blocks, in_width), F32)
-        for j in range(0, pairs, 2):
-            left = jnp.concatenate(
-                [
-                    owner[:, i : i + 1] * returned[i : i + 1]
-                    for i in (j, j + 1)
-                ],
-                axis=1,
-            ).astype(BF16)
-            total = total + lax.dot_general(
-                left, wide(j), (((1,), (1,)), ((), ())), preferred_element_type=F32
-            )
-        xbuf[...] = jnp.concatenate(
-            [total[i * rows : (i + 1) * rows] for i in range(in_per_row)], axis=1
-        )
-        x_copy().start()
 
     wait_rows(3, p2)
     stores[3].start()
@@ -617,24 +569,29 @@
     def _():
         for t in range(n_gx):
             y_copy(t).wait_send()
-        x_copy().wait_recv()
-        sbuf[...] = xbuf[...]
+        for t in range(n_gx):
+            pltpu.make_async_remote_copy(
+                src_ref=tsend,
+                dst_ref=trecv.at[t],
+                send_sem=t_send.at[t],
+                recv_sem=t_recv.at[t],
+                device_id=(1, t, b),
+                device_id_type=MESH,
+            ).wait_recv()
+        returned_copy = pltpu.make_async_copy(trecv, returned, surface_sem)
+        returned_copy.start()
+        returned_copy.wait()
 
     @pl.when(sec == 1)
     def _():
+        surface_copy = pltpu.make_async_copy(sbuf, surface.at[0], surface_sem)
+        surface_copy.start()
         for t in range(n_gx):
-
-            @pl.when(t != a)
-            def _():
-                t_copy(t).wait_send()
-
-        x_copy().wait_send()
-
-    surface_copy = pltpu.make_async_copy(sbuf, surface.at[0], surface_sem)
-    surface_copy.start()
+            t_copy(t).wait_send()
+        surface_copy.wait()
+
     for copy in stores:
         copy.wait()
-    surface_copy.wait()
 
 
 def last_kernel(
@@ -643,24 +600,36 @@
     v_in,
     mask_in,
     surface_in,
+    returned_in,
+    tile_hbm,
+    source_hbm,
+    target_hbm,
+    weights,
     final,
     surface,
     p,
     u,
     v,
     mask,
+    returned,
+    tile_in,
+    source_in,
+    target_in,
+    wbuf,
+    sbuf,
     out,
     sem,
     out_sem,
     small_sem,
+    w_sem,
 ):
+    sec = lax.axis_index("sec")
     rows, levels, width = u_in.shape
     tiles = width // LANES
     parts = rows // 4
     half = 8
 
     mask_copy = pltpu.make_async_copy(mask_in, mask, small_sem.at[0])
-    surface_copy = pltpu.make_async_copy(surface_in, surface, small_sem.at[1])
     mask_copy.start()
     loads = []
     for k in range(parts):
@@ -681,7 +650,31 @@
         )
         for copy in loads[-1]:
             copy.start()
-    surface_copy.start()
+    small = [
+        pltpu.make_async_copy(src, dst, small_sem.at[2 + i])
+        for i, (src, dst) in enumerate(
+            (
+                (returned_in, returned),
+                (tile_hbm, tile_in),
+                (source_hbm, source_in),
+                (target_hbm, target_in),
+            )
+        )
+    ]
+    pairs, in_width, out_width = wbuf.shape
+    per_chunk = pairs // CHUNKS
+
+    def load_weights(i):
+        group = pl.ds(i * per_chunk, per_chunk)
+        return pltpu.make_async_copy(weights.at[0, 0, group], wbuf.at[group], w_sem.at[i])
+
+    @pl.when(sec == 0)
+    def _():
+        for copy in small:
+            copy.start()
+        for i in range(CHUNKS):
+            load_weights(i).start()
+
     mask_copy.wait()
 
     def store(h, f, i):
@@ -715,9 +708,45 @@
             h = (4 * k + 4) // half - 1
             for copy in stores[h * per_half : (h + 1) * per_half]:
                 copy.start()
+
+    @pl.when(sec == 0)
+    def _():
+        for copy in small:
+            copy.wait()
+        in_per_row, out_per_row = width // in_width, width // out_width
+        in_blocks, out_blocks = rows * in_per_row, rows * out_per_row
+        slots = returned.shape[0] * out_blocks
+        slot_col = upright(wide_row(tile_in) * out_blocks + wide_row(target_in))
+        slot = slot_key(iota((pairs, slots), 1), out_blocks, rows, out_per_row)
+        picking = (slot == slot_col).astype(F32).astype(BF16)
+        per_pair = dot(picking, returned[...].reshape(slots, out_width))
+        key = block_key(iota((in_blocks, pairs), 0), rows, in_per_row).astype(F32)
+        owner = (key == wide_row(source_in)).astype(F32)
+        total = jnp.zeros((in_blocks, in_width), F32)
+        for j in range(0, pairs, 2):
+            if j % per_chunk == 0:
+                load_weights(j // per_chunk).wait()
+            left = jnp.concatenate(
+                [owner[:, i : i + 1] * per_pair[i : i + 1] for i in (j, j + 1)], axis=1
+            ).astype(BF16)
+            total = total + lax.dot_general(
+                left, wide(wbuf, j), (((1,), (1,)), ((), ())), preferred_element_type=F32
+            )
+        sbuf[...] = jnp.concatenate(
+            [total[i * rows : (i + 1) * rows] for i in range(in_per_row)], axis=1
+        )
+        surface_copy = pltpu.make_async_copy(sbuf, surface.at[0], small_sem.at[1])
+        surface_copy.start()
+        surface_copy.wait()
+
+    @pl.when(sec == 1)
+    def _():
+        surface_copy = pltpu.make_async_copy(surface_in, surface, small_sem.at[1])
+        surface_copy.start()
+        surface_copy.wait()
+
     for copy in stores:
         copy.wait()
-    surface_copy.wait()
 
 
 def local(n_gx, n_gy, *args):
@@ -736,16 +765,17 @@
     tall = pltpu.VMEM((rows + 2, levels, span), F32)
     ext = pltpu.VMEM((rows, levels, LANES), F32)
     params = dict(has_side_effects=True, vmem_limit_bytes=62 * 2**20)
-    p2, u1, v1, surface = pl.pallas_call(
+    p2, u1, v1, surface, returned = pl.pallas_call(
         functools.partial(kernel, n_gx, n_gy),
         out_shape=(
             jax.ShapeDtypeStruct((rows + 2, levels, span), F32),
             jax.ShapeDtypeStruct((rows, levels, width), F32),
             jax.ShapeDtypeStruct((rows, levels, width), F32),
             jax.ShapeDtypeStruct(temp.shape, F32),
+            jax.ShapeDtypeStruct((n_gx, out_blocks, out_width), BF16),
         ),
         in_specs=[hbm] * 11,
-        out_specs=(free,) * 4,
+        out_specs=(free,) * 5,
         scratch_shapes=[
             pltpu.VMEM(speed.shape, F32),
             pltpu.VMEM(mask.shape, jnp.int32),
@@ -777,8 +807,8 @@
             pltpu.VMEM((2, rows, LANES), jnp.int32),
             pltpu.VMEM((n_gx, out_blocks, out_width), BF16),
             pltpu.VMEM((n_gx, out_blocks, out_width), BF16),
+            pltpu.VMEM((out_blocks, out_width), BF16),
             pltpu.VMEM((n_gx, out_blocks, out_width), BF16),
-            pltpu.VMEM((rows, width), F32),
             pltpu.VMEM((rows, width), F32),
             dma((fields, width // LANES)),
             dma((9,)),
@@ -792,8 +822,6 @@
             dma((n_gx,)),
             dma((n_gx,)),
             dma((n_gx,)),
-            dma(()),
-            dma(()),
             dma((5,)),
         ],
         compiler_params=pltpu.CompilerParams(collective_id=0, **params),
@@ -804,20 +832,27 @@
             jax.ShapeDtypeStruct(state.shape, F32),
             jax.ShapeDtypeStruct(temp.shape, F32),
         ),
-        in_specs=[hbm] * 5,
+        in_specs=[hbm] * 10,
         out_specs=(free, free),
         scratch_shapes=[
             tall,
             pltpu.VMEM((rows, levels, width), F32),
             pltpu.VMEM((rows, levels, width), F32),
             pltpu.VMEM(mask.shape, jnp.int32),
+            pltpu.VMEM(returned.shape, BF16),
+            pltpu.VMEM(tile.shape, jnp.int32),
+            pltpu.VMEM(source.shape, jnp.int32),
+            pltpu.VMEM(target.shape, jnp.int32),
+            pltpu.VMEM((pairs, in_width, out_width), BF16),
+            pltpu.VMEM((rows, width), F32),
             pltpu.VMEM((rows // 8, fields, width // LANES, levels, 8, LANES), F32),
             dma((rows // 4, 3)),
             dma((rows // 8, fields, width // LANES)),
-            dma((2,)),
+            dma((6,)),
+            dma((CHUNKS,)),
         ],
         compiler_params=pltpu.CompilerParams(**params),
-    )(p2, u1, v1, mask, surface)
+    )(p2, u1, v1, mask, surface, returned, tile, source, target, weights)
 
 
 def solution(mesh):

time: 29.4 us -> 31.4 us (1.068)
  Pallas kernels: 28.7 us -> 30.6 us
    pallas_call x1, Pallas kernels: 4.4 us -> 7.16 us  [local(): pl.pallas_call(last_kernel, out_shape=(jax.ShapeDtypeStruct(state.shape,...]
    pallas_call x1, Pallas kernels: 24.3 us -> 23.4 us  [local(): pl.pallas_call(functools.partial(kernel, n_gx, n_gy), out_shape=(jax.Shap...]
where the time goes in v4:
time: 31.4 us; the launch traced here: 31.3 us
  Pallas kernels  30.6 us (97%)
  between operations  0.64 us (2%)
    pallas_call x1, Pallas kernels, local(): pl.pallas_call(functools.partial(kernel, n_gx, n_gy), out_shape=(jax.Shap...  23.4 us
    pallas_call x1, Pallas kernels, local(): pl.pallas_call(last_kernel, out_shape=(jax.ShapeDtypeStruct(state.shape,...  7.16 us

profile of v4, /device:TPU:0, one launch (start us, length us, event | category | flops | bytes accessed | tf_op | source)
XLA Modules:
  0.0 31.3 jit_solution(5132761203971679620)
XLA Ops:
  0.6 23.4 %shard_map.122 = (f32[18,32,640]{2,1,0:T(8,128)}, f32[16,32,512]{2,1,0:T(8,128)}, f32[16,32,512]{2,1,0:T(8,128)}, f32[1,16,512]{2,1,0:T(8,128)}, bf16[4,64,128]{2,1,0:T(8,128)(2,1)}) custom-call(f32[1,3,32,16,512]{4,3,2,1,0:T(8,128)} %state.1, f32[1,16,512]{2,1,0:T(8,128)} %speed_in.1, s32[1,16,512]{2,1,0:T(8,128)} %mask_in.3, f32[1,32,32]{2,1,0:T(8,128)} %vertical_in.1, ...), custom_call_target="tpu_custom_call" | custom-call | tf_op jit(solution)/shard_map/pallas_call | solution.py:768
  24.1 7.2 %shard_map.123 = (f32[1,3,32,16,512]{4,3,2,1,0:T(8,128)}, f32[1,16,512]{2,1,0:T(8,128)}) custom-call(f32[18,32,640]{2,1,0:T(8,128)} %get-tuple-element.7.p_in, f32[16,32,512]{2,1,0:T(8,128)} %get-tuple-element.8.u_in, f32[16,32,512]{2,1,0:T(8,128)} %get-tuple-element.9.v_in, s32[1,16,512]{2,1,0:T(8,128)} %mask_in.3, ...), custom_call_target="tpu_custom_call" | custom-call | tf_op jit(solution)/shard_map/pallas_call | solution.py:829

commit v5 on v4

--- a/solution.py
+++ b/solution.py
@@ -12,10 +12,10 @@
 BF16 = jnp.bfloat16
 LANES = 128
 CHUNKS = 8
-STAGES = 4
+EXCHANGES = 2
 MARGIN = 4
 P_FIELD, U_FIELD, V_FIELD = 0, 1, 2
-SPEED, MASK, P_COLS, V_COLS, U_COLS, U_BEFORE, U_AFTER = range(7)
+SPEED, MASK, P_COLS, V_COLS, U_COLS = range(5)
 
 
 def iota(shape, axis):
@@ -183,23 +183,16 @@
 
     row_ok = (a > 0, a < n_gx - 1)
     col_ok = (b > 0, b < n_gy - 1)
-    both_ok = [[jnp.logical_and(r, c) for c in col_ok] for r in row_ok]
 
     for side in range(2):
-        for dx in (-1, 0, 1):
-            near = col_ok[side] if dx == 0 else both_ok[(dx + 1) // 2][side]
-
-            @pl.when(near)
-            def _(side=side, dx=dx):
-                pl.semaphore_signal(
-                    barrier,
-                    inc=1,
-                    device_id=(sec, a + dx, b + 2 * side - 1),
-                    device_id_type=MESH,
-                )
+
+        @pl.when(col_ok[side])
+        def _(side=side):
+            pl.semaphore_signal(
+                barrier, inc=1, device_id=(sec, a, b + 2 * side - 1), device_id_type=MESH
+            )
 
     beside = (b > 0).astype(jnp.int32) + (b < n_gy - 1).astype(jnp.int32)
-    beside = beside * (1 + (a > 0).astype(jnp.int32) + (a < n_gx - 1).astype(jnp.int32))
 
     for side in range(2):
 
@@ -207,27 +200,22 @@
         def _(side=side):
             for buf in (u0, p1, u1, p2):
                 buf[side * (rows + 1)] = jnp.zeros(buf.shape[1:], F32)
-            for other in range(2):
-                u_recv[2 * side, other] = jnp.zeros((levels, LANES), F32)
 
         @pl.when(jnp.logical_not(col_ok[side]))
         def _(side=side):
-            for dx in range(3):
-                u_recv[dx, side] = jnp.zeros((levels, LANES), F32)
+            u_recv[side] = jnp.zeros((levels, LANES), F32)
             v_recv[side] = jnp.zeros((levels, LANES), F32)
             p_recv[side] = jnp.zeros((levels, LANES), F32)
             speed_recv[side] = jnp.zeros((rows, LANES), F32)
             mask_recv[side] = jnp.zeros((rows, LANES), jnp.int32)
 
-    def row_copy(stage, side):
-        src, dst = rowsend.at[stage, side], rowrecv.at[stage, 1 - side]
-        if stage == 0:
-            src, dst = src.at[:, pl.ds(0, width)], dst.at[:, pl.ds(0, width)]
+    def row_copy(exchange, side):
+        part = pl.ds(0, 2 * levels if exchange else rowsend.shape[2])
         return pltpu.make_async_remote_copy(
-            src_ref=src,
-            dst_ref=dst,
-            send_sem=row_send.at[stage, side],
-            recv_sem=row_recv.at[stage, side],
+            src_ref=rowsend.at[exchange, side, part],
+            dst_ref=rowrecv.at[exchange, 1 - side, part],
+            send_sem=row_send.at[exchange, side],
+            recv_sem=row_recv.at[exchange, side],
             device_id=(sec, a - 1 if side == 0 else a + 1, b),
             device_id_type=MESH,
         )
@@ -240,79 +228,77 @@
             MASK: (mask.at[0, :, edge], mask_recv.at[other]),
             P_COLS: (colsend.at[P_FIELD, side], p_recv.at[other]),
             V_COLS: (colsend.at[V_FIELD, side], v_recv.at[other]),
-            U_COLS: (colsend.at[U_FIELD, side], u_recv.at[1, other]),
-            U_BEFORE: (colsend.at[U_FIELD, side], u_recv.at[2, other]),
-            U_AFTER: (colsend.at[U_FIELD, side], u_recv.at[0, other]),
+            U_COLS: (colsend.at[U_FIELD, side], u_recv.at[other]),
         }[kind]
-        to = {U_BEFORE: a - 1, U_AFTER: a + 1}.get(kind, a)
         return pltpu.make_async_remote_copy(
             src_ref=src,
             dst_ref=dst,
             send_sem=col_send.at[kind, side],
             recv_sem=col_recv.at[kind, side],
-            device_id=(sec, to, b - 1 if side == 0 else b + 1),
+            device_id=(sec, a, b - 1 if side == 0 else b + 1),
             device_id_type=MESH,
         )
-
-    def col_sends(kind, side):
-        return {U_BEFORE: both_ok[0], U_AFTER: both_ok[1]}.get(kind, col_ok)[side]
-
-    def col_comes(kind, side):
-        return {U_BEFORE: both_ok[1], U_AFTER: both_ok[0]}.get(kind, col_ok)[side]
-
-    def send_rows(stage, buf):
-        span = width if stage == 0 else width + LANES
-        for side in range(2):
-
-            @pl.when(row_ok[side])
-            def _(side=side):
-                edge = buf[rows if side else 1]
-                rowsend[stage, side, :, :span] = edge[:, :span].astype(BF16)
-                row_copy(stage, side).start()
 
     def send_cols(*kinds):
         for kind in kinds:
             for side in range(2):
 
-                @pl.when(col_sends(kind, side))
+                @pl.when(col_ok[side])
                 def _(side=side, kind=kind):
                     col_copy(kind, side).start()
 
     def wait_cols():
-        for kind in range(7):
+        for kind in range(5):
             for side in range(2):
 
-                @pl.when(col_comes(kind, side))
+                @pl.when(col_ok[side])
                 def _(side=side, kind=kind):
                     col_copy(kind, 1 - side).wait_recv()
 
-    def wait_rows(stage, buf):
+    def wait_sent():
+        for side in range(2):
+            for kind in range(5):
+
+                @pl.when(col_ok[side])
+                def _(side=side, kind=kind):
+                    col_copy(kind, side).wait_send()
+
+            for exchange in range(EXCHANGES):
+
+                @pl.when(row_ok[side])
+                def _(side=side, exchange=exchange):
+                    row_copy(exchange, side).wait_send()
+
+    def send_edges(exchange, u_buf, p_row, v_row):
         for side in range(2):
 
             @pl.when(row_ok[side])
             def _(side=side):
-                row_copy(stage, 1 - side).wait_recv()
+                x = side * (rows - 1)
+                inner = -u_buf[x] if side else u_buf[x + 2]
+                c = c_wide[x : x + 1, :]
+                partial = p_row(x) - c * (inner + along_y(v_row(x)))
+                rowsend[exchange, side, :levels] = u_buf[x + 1].astype(BF16)
+                rowsend[exchange, side, levels : 2 * levels] = partial.astype(BF16)
+                if exchange == 0:
+                    high, low = [piece.astype(F32) for piece in split(c, 2)]
+                    at = iota((rowsend.shape[2] - 2 * levels, c.shape[1]), 0)
+                    both = jnp.where(at == 0, high, jnp.where(at == 1, low, 0.0))
+                    rowsend[exchange, side, 2 * levels :] = both.astype(BF16)
+                row_copy(exchange, side).start()
+
+    def wait_edges(exchange, u_buf, p_buf):
+        for side in range(2):
+
+            @pl.when(row_ok[side])
+            def _(side=side):
+                row_copy(exchange, 1 - side).wait_recv()
                 at = rows + 1 if side else 0
-                if stage == 0:
-                    buf[at, :, :width] = rowrecv[stage, side, :, :width].astype(F32)
-                    near = u_recv.at[2 * side]
-                    buf[at, :, width:] = margin(near, 0 if side else rows - 1)
-                else:
-                    buf[at] = rowrecv[stage, side].astype(F32)
-
-    def wait_sent():
-        for side in range(2):
-            for kind in range(7):
-
-                @pl.when(col_sends(kind, side))
-                def _(side=side, kind=kind):
-                    col_copy(kind, side).wait_send()
-
-            for stage in range(STAGES):
-
-                @pl.when(row_ok[side])
-                def _(side=side, stage=stage):
-                    row_copy(stage, side).wait_send()
+                u_buf[at] = rowrecv[exchange, side, :levels].astype(F32)
+                partial = rowrecv[exchange, side, levels : 2 * levels].astype(F32)
+                c = rowrecv[0, side, 2 * levels :].astype(F32)
+                term = (c[0:1] + c[1:2]) * u_buf[rows if side else 1]
+                p_buf[at] = mix(partial + term if side else partial - term)
 
     lane = iota((levels, LANES), 1)
 
@@ -370,30 +356,20 @@
         divergence = (u_buf[x + 2] - u_buf[x]) + along_y(v)
         return mix(p - c_wide[pl.ds(x, 1), :] * divergence)
 
-    def sweep(row, after_edges):
-        def edge(i, c):
-            row(i * (rows - 1))
-            return c
-
-        lax.fori_loop(0, 2, edge, 0)
-        after_edges()
-        inner = rows - 2
-        step = next(k for k in (7, 6, 5, 4, 3, 2, 1) if inner % k == 0)
+    def sweep(row, first, count):
+        step = next(k for k in (8, 7, 6, 5, 4, 3, 2, 1) if count % k == 0)
 
         def several(i, c):
             for k in range(step):
-                row(i * step + 1 + k)
+                row(first + i * step + k)
             return c
 
-        lax.fori_loop(0, inner // step, several, 0)
+        lax.fori_loop(0, count // step, several, 0)
 
     loaded(U_FIELD)
-    u0[1, :, :width] = column(U_FIELD, 0)
-    u0[rows, :, :width] = column(U_FIELD, rows - 1)
+    pack_all(U_FIELD)
     pl.semaphore_wait(barrier, 2 * n_gx - 1 + beside)
-    send_rows(0, u0)
-    pack_all(U_FIELD)
-    send_cols(U_COLS, U_BEFORE, U_AFTER)
+    send_cols(U_COLS)
     loaded(V_FIELD)
     pack_all(V_FIELD)
     send_cols(V_COLS)
@@ -470,20 +446,18 @@
         for t in range(n_gx):
             y_copy(t).start()
 
-    def fill(x, c):
+    def fill(x):
         u0[x + 1, :, :width] = column(U_FIELD, x)
-        return c
-
-    lax.fori_loop(1, rows - 1, fill, 0)
+
+    sweep(fill, 0, rows)
     wait_cols()
 
-    def fill_margins(x, c):
-        u0[x + 1, :, width:] = margin(u_recv.at[1], x)
+    def fill_margins(x):
+        u0[x + 1, :, width:] = margin(u_recv, x)
         v_ext[x] = margin(v_recv, x)
         p_ext[x] = margin(p_recv, x)
-        return c
-
-    lax.fori_loop(0, rows, fill_margins, 0)
+
+    sweep(fill_margins, 0, rows)
     across = iota((rows, LANES), 1)
 
     def around(pair):
@@ -494,34 +468,43 @@
     c_wide[:, width:] = around(speed_recv[...])
     w_wide[:, :width] = mask[0].astype(F32)
     w_wide[:, width:] = around(mask_recv[...].astype(F32))
-    wait_rows(0, u0)
 
     def wide_column(f, ext, x):
         return jnp.concatenate([column(f, x), ext[x]], axis=1)
 
+    def p_first(x):
+        return wide_column(P_FIELD, p_ext, x)
+
+    def v_first(x):
+        return wide_column(V_FIELD, v_ext, x)
+
     def first_pressure(x):
-        p = wide_column(P_FIELD, p_ext, x)
-        p1[x + 1] = pressure_row(x, p, u0, wide_column(V_FIELD, v_ext, x))
-
-    sweep(first_pressure, lambda: send_rows(1, p1))
-    wait_rows(1, p1)
+        p1[x + 1] = pressure_row(x, p_first(x), u0, v_first(x))
+
+    send_edges(0, u0, p_first, v_first)
+    sweep(first_pressure, 1, rows - 2)
+    wait_edges(0, u0, p1)
+    first_pressure(0)
+    first_pressure(rows - 1)
 
     def first_velocity(x):
         w = w_wide[pl.ds(x, 1), :]
         u1[x + 1] = w * (u0[x + 1] - 0.5 * (p1[x + 2] - p1[x]))
-        v1[x] = w * (wide_column(V_FIELD, v_ext, x) - 0.5 * along_y(p1[x + 1]))
-
-    sweep(first_velocity, lambda: send_rows(2, u1))
+        v1[x] = w * (v_first(x) - 0.5 * along_y(p1[x + 1]))
+
+    for x in (0, 1, rows - 2, rows - 1):
+        first_velocity(x)
+    send_edges(1, u1, lambda x: p1[x + 1], lambda x: v1[x])
+    sweep(first_velocity, 2, rows - 4)
 
     near = pl.ds(0, width)
-    inner = pl.ds(1, rows)
     stores = [
-        pltpu.make_async_copy(u1.at[inner, :, near], u1_out, out_sem.at[0]),
+        pltpu.make_async_copy(u1.at[pl.ds(1, rows), :, near], u1_out, out_sem.at[0]),
         pltpu.make_async_copy(v1.at[:, :, near], v1_out, out_sem.at[1]),
-        pltpu.make_async_copy(p2.at[inner], p2_out.at[inner], out_sem.at[2]),
-        pltpu.make_async_copy(p2.at[0], p2_out.at[0], out_sem.at[3]),
-        pltpu.make_async_copy(p2.at[rows + 1], p2_out.at[rows + 1], out_sem.at[4]),
     ]
+    for i, (first, count) in enumerate(((2, rows - 2), (0, 2), (rows, 2))):
+        part = pl.ds(first, count)
+        stores.append(pltpu.make_async_copy(p2.at[part], p2_out.at[part], out_sem.at[2 + i]))
     stores[0].start()
     stores[1].start()
 
@@ -552,15 +535,14 @@
             [ocean[i * rows : (i + 1) * rows] for i in range(out_per_row)], axis=1
         )
 
-    wait_rows(2, u1)
-
     def second_pressure(x):
         p2[x + 1] = pressure_row(x, p1[x + 1], u1, v1[x])
 
-    sweep(second_pressure, lambda: send_rows(3, p2))
+    sweep(second_pressure, 1, rows - 2)
     stores[2].start()
-
-    wait_rows(3, p2)
+    wait_edges(1, u1, p2)
+    second_pressure(0)
+    second_pressure(rows - 1)
     stores[3].start()
     stores[4].start()
     wait_sent()
@@ -797,10 +779,10 @@
             ext,
             pltpu.VMEM((rows, span), F32),
             pltpu.VMEM((rows, span), F32),
-            pltpu.VMEM((STAGES, 2, levels, span), BF16),
-            pltpu.VMEM((STAGES, 2, levels, span), BF16),
+            pltpu.VMEM((EXCHANGES, 2, 2 * levels + 16, span), BF16),
+            pltpu.VMEM((EXCHANGES, 2, 2 * levels + 16, span), BF16),
             pltpu.VMEM((fields, 2, levels, LANES), F32),
-            pltpu.VMEM((3, 2, levels, LANES), F32),
+            pltpu.VMEM((2, levels, LANES), F32),
             pltpu.VMEM((2, levels, LANES), F32),
             pltpu.VMEM((2, levels, LANES), F32),
             pltpu.VMEM((2, rows, LANES), F32),
@@ -814,10 +796,10 @@
             dma((9,)),
             dma(()),
             dma((CHUNKS,)),
-            dma((STAGES, 2)),
-            dma((STAGES, 2)),
-            dma((7, 2)),
-            dma((7, 2)),
+            dma((EXCHANGES, 2)),
+            dma((EXCHANGES, 2)),
+            dma((5, 2)),
+            dma((5, 2)),
             dma((n_gx,)),
             dma((n_gx,)),
             dma((n_gx,)),

time: 31.4 us -> 29.1 us (0.927)
  Pallas kernels: 30.6 us -> 28.3 us
    pallas_call x1, Pallas kernels: 23.4 us -> 21.1 us  [local(): pl.pallas_call(functools.partial(kernel, n_gx, n_gy), out_shape=(jax.Shap...]
where the time goes in v5:
time: 29.1 us; the launch traced here: 28.9 us
  Pallas kernels  28.3 us (97%)
  between operations  0.64 us (2%)
    pallas_call x1, Pallas kernels, local(): pl.pallas_call(functools.partial(kernel, n_gx, n_gy), out_shape=(jax.Shap...  21.1 us
    pallas_call x1, Pallas kernels, local(): pl.pallas_call(last_kernel, out_shape=(jax.ShapeDtypeStruct(state.shape,...  7.16 us

profile of v5, /device:TPU:0, one launch (start us, length us, event | category | flops | bytes accessed | tf_op | source)
XLA Modules:
  0.0 28.9 jit_solution(17333948779878426137)
XLA Ops:
  0.6 21.1 %shard_map.122 = (f32[18,32,640]{2,1,0:T(8,128)}, f32[16,32,512]{2,1,0:T(8,128)}, f32[16,32,512]{2,1,0:T(8,128)}, f32[1,16,512]{2,1,0:T(8,128)}, bf16[4,64,128]{2,1,0:T(8,128)(2,1)}) custom-call(f32[1,3,32,16,512]{4,3,2,1,0:T(8,128)} %state.1, f32[1,16,512]{2,1,0:T(8,128)} %speed_in.1, s32[1,16,512]{2,1,0:T(8,128)} %mask_in.3, f32[1,32,32]{2,1,0:T(8,128)} %vertical_in.1, ...), custom_call_target="tpu_custom_call" | custom-call | tf_op jit(solution)/shard_map/pallas_call | solution.py:750
  21.7 7.2 %shard_map.123 = (f32[1,3,32,16,512]{4,3,2,1,0:T(8,128)}, f32[1,16,512]{2,1,0:T(8,128)}) custom-call(f32[18,32,640]{2,1,0:T(8,128)} %get-tuple-element.7.p_in, f32[16,32,512]{2,1,0:T(8,128)} %get-tuple-element.8.u_in, f32[16,32,512]{2,1,0:T(8,128)} %get-tuple-element.9.v_in, s32[1,16,512]{2,1,0:T(8,128)} %mask_in.3, ...), custom_call_target="tpu_custom_call" | custom-call | tf_op jit(solution)/shard_map/pallas_call | solution.py:811

commit v6 on v5

--- a/solution.py
+++ b/solution.py
@@ -110,6 +110,8 @@
     tsend,
     trecv,
     sbuf,
+    picked,
+    heated,
     load_sem,
     small_sem,
     surface_sem,
@@ -406,8 +408,7 @@
             device_id_type=MESH,
         )
 
-    @pl.when(sec == 0)
-    def _():
+    def take_fluxes():
         drivers = [
             jnp.concatenate([raw[f, i, 0] for i in range(tiles)], axis=1) for f in range(3)
         ] + [temp[0]]
@@ -424,27 +425,37 @@
         source_col = upright(wide_row(source_in))
         key = block_key(iota((pairs, in_blocks), 1), rows, in_per_row).astype(F32)
         picking = (source_col == key).astype(F32).astype(BF16)
-        high, low = [dot(picking, piece) for piece in split(blocks, 2)]
+        for i, piece in enumerate(split(blocks, 2)):
+            picked[i] = dot(picking, piece)
+
+    def regrid(first, last):
         sub = iota((8, out_width), 0)
-        groups = []
-        for g in range(pairs // 8):
+        for g in range(first, last):
             if g % (per_chunk // 8) == 0:
                 load_weights(g * 8 // per_chunk).wait()
             part = slice(8 * g, 8 * g + 8)
-            left = jnp.concatenate([high[part], low[part]], axis=0).astype(BF16)
+            left = jnp.concatenate([picked[0, part], picked[1, part]], axis=0).astype(BF16)
             group = jnp.zeros((8, out_width), F32)
             for i in range(0, 8, 2):
                 both = dot(left, wide(wbuf, 8 * g + i))
                 both = both[:8] + both[8:]
                 group = jnp.where(sub == i, both[:, :out_width], group)
                 group = jnp.where(sub == i + 1, both[:, out_width:], group)
-            groups.append(group)
-        heated = jnp.concatenate(groups, axis=0)
+            heated[part] = group
+
+    def send_sums():
         placing = (slot_key(iota((slots, pairs), 0), out_blocks, rows, out_per_row) == slot_row).astype(F32).astype(BF16)
-        dense = sum(dot(placing, piece) for piece in split(heated, 3))
+        dense = sum(dot(placing, piece) for piece in split(heated[...], 3))
         ybuf[...] = dense.astype(BF16).reshape(n_gx, out_blocks, out_width)
         for t in range(n_gx):
             y_copy(t).start()
+
+    halfway = pairs // 16
+
+    @pl.when(sec == 0)
+    def _():
+        take_fluxes()
+        regrid(0, halfway)
 
     def fill(x):
         u0[x + 1, :, :width] = column(U_FIELD, x)
@@ -482,6 +493,12 @@
         p1[x + 1] = pressure_row(x, p_first(x), u0, v_first(x))
 
     send_edges(0, u0, p_first, v_first)
+
+    @pl.when(sec == 0)
+    def _():
+        regrid(halfway, pairs // 8)
+        send_sums()
+
     sweep(first_pressure, 1, rows - 2)
     wait_edges(0, u0, p1)
     first_pressure(0)
@@ -534,6 +551,7 @@
         sbuf[...] = jnp.concatenate(
             [ocean[i * rows : (i + 1) * rows] for i in range(out_per_row)], axis=1
         )
+        pltpu.make_async_copy(sbuf, surface.at[0], surface_sem).start()
 
     def second_pressure(x):
         p2[x + 1] = pressure_row(x, p1[x + 1], u1, v1[x])
@@ -545,12 +563,9 @@
     second_pressure(rows - 1)
     stores[3].start()
     stores[4].start()
-    wait_sent()
 
     @pl.when(sec == 0)
     def _():
-        for t in range(n_gx):
-            y_copy(t).wait_send()
         for t in range(n_gx):
             pltpu.make_async_remote_copy(
                 src_ref=tsend,
@@ -560,17 +575,21 @@
                 device_id=(1, t, b),
                 device_id_type=MESH,
             ).wait_recv()
-        returned_copy = pltpu.make_async_copy(trecv, returned, surface_sem)
-        returned_copy.start()
-        returned_copy.wait()
+        pltpu.make_async_copy(trecv, returned, surface_sem).start()
+
+    wait_sent()
+
+    @pl.when(sec == 0)
+    def _():
+        for t in range(n_gx):
+            y_copy(t).wait_send()
+        pltpu.make_async_copy(trecv, returned, surface_sem).wait()
 
     @pl.when(sec == 1)
     def _():
-        surface_copy = pltpu.make_async_copy(sbuf, surface.at[0], surface_sem)
-        surface_copy.start()
         for t in range(n_gx):
             t_copy(t).wait_send()
-        surface_copy.wait()
+        pltpu.make_async_copy(sbuf, surface.at[0], surface_sem).wait()
 
     for copy in stores:
         copy.wait()
@@ -657,6 +676,10 @@
         for i in range(CHUNKS):
             load_weights(i).start()
 
+    @pl.when(sec == 1)
+    def _():
+        pltpu.make_async_copy(surface_in, surface, small_sem.at[1]).start()
+
     mask_copy.wait()
 
     def store(h, f, i):
@@ -723,9 +746,7 @@
 
     @pl.when(sec == 1)
     def _():
-        surface_copy = pltpu.make_async_copy(surface_in, surface, small_sem.at[1])
-        surface_copy.start()
-        surface_copy.wait()
+        pltpu.make_async_copy(surface_in, surface, small_sem.at[1]).wait()
 
     for copy in stores:
         copy.wait()
@@ -792,6 +813,8 @@
             pltpu.VMEM((out_blocks, out_width), BF16),
             pltpu.VMEM((n_gx, out_blocks, out_width), BF16),
             pltpu.VMEM((rows, width), F32),
+            pltpu.VMEM((2, pairs, in_width), F32),
+            pltpu.VMEM((pairs, out_width), F32),
             dma((fields, width // LANES)),
             dma((9,)),
             dma(()),

time: 29.1 us -> 29.2 us (level)
  no operation moved by 1% of the time
where the time goes in v6:
time: 29.2 us; the launch traced here: 29.1 us
  Pallas kernels  28.4 us (97%)
  between operations  0.64 us (2%)
    pallas_call x1, Pallas kernels, local(): pl.pallas_call(functools.partial(kernel, n_gx, n_gy), out_shape=(jax.Shap...  21.3 us
    pallas_call x1, Pallas kernels, local(): pl.pallas_call(last_kernel, out_shape=(jax.ShapeDtypeStruct(state.shape,...  7.16 us

profile of v6, /device:TPU:0, one launch (start us, length us, event | category | flops | bytes accessed | tf_op | source)
XLA Modules:
  0.0 29.1 jit_solution(17404429517131222276)
XLA Ops:
  0.6 21.3 %shard_map.122 = (f32[18,32,640]{2,1,0:T(8,128)}, f32[16,32,512]{2,1,0:T(8,128)}, f32[16,32,512]{2,1,0:T(8,128)}, f32[1,16,512]{2,1,0:T(8,128)}, bf16[4,64,128]{2,1,0:T(8,128)(2,1)}) custom-call(f32[1,3,32,16,512]{4,3,2,1,0:T(8,128)} %state.1, f32[1,16,512]{2,1,0:T(8,128)} %speed_in.1, s32[1,16,512]{2,1,0:T(8,128)} %mask_in.3, f32[1,32,32]{2,1,0:T(8,128)} %vertical_in.1, ...), custom_call_target="tpu_custom_call" | custom-call | tf_op jit(solution)/shard_map/pallas_call | solution.py:771
  21.9 7.2 %shard_map.123 = (f32[1,3,32,16,512]{4,3,2,1,0:T(8,128)}, f32[1,16,512]{2,1,0:T(8,128)}) custom-call(f32[18,32,640]{2,1,0:T(8,128)} %get-tuple-element.7.p_in, f32[16,32,512]{2,1,0:T(8,128)} %get-tuple-element.8.u_in, f32[16,32,512]{2,1,0:T(8,128)} %get-tuple-element.9.v_in, s32[1,16,512]{2,1,0:T(8,128)} %mask_in.3, ...), custom_call_target="tpu_custom_call" | custom-call | tf_op jit(solution)/shard_map/pallas_call | solution.py:834
